TPU v7x, 512 devices: a whole 4x4x16 slice. The times are simulated.
512 devices in a mesh: gx: 8 (over y, z_hi), gy: 8 (over z_lo), gz: 8 (over x, core).
Axes of the slice: x: 4, y: 4, z: 16 (z_hi: 2, z_lo: 8; z = z_hi * 8 + z_lo), core: 2. Of those that a mesh axis runs over, the one named last changes fastest.
Arguments:
- right_side: float32 [4, 64, 64, 1024], P(None, 'gx', 'gy', 'gz'), may hold values from -5 to 5.2
- affinity: float32 [3, 64, 64, 1024], P(None, 'gx', 'gy', 'gz'), may hold values from 0.05 to 1
Outputs:
- correction: float32 [4, 64, 64, 1024], P(None, 'gx', 'gy', 'gz')
All inputs are finite; a program needn't handle non-finite values.
Results may differ from a plain program's by a relative error of at most 0.0001.
Values sent between devices are 32-bit elements; how exact they have to be, the bound alone decides.
A program may use at most 128 MiB of HBM per device.

v0:
```python
import jax
import jax.numpy as jnp
from jax import lax
from jax.sharding import PartitionSpec as P

DEGREE = 3
COARSE_DEGREE = 8


SPECTRAL_SHIFT = 0.02
SMOOTH_LOWER = 0.5
SMOOTH_UPPER = 2.0 + SPECTRAL_SHIFT


def extended(block, sides, width):
    for axis, dim in sides:
        count = lax.axis_size(axis)
        forward = [(i, i + 1) for i in range(count - 1)]
        backward = [(target, source) for source, target in forward]
        low = lax.ppermute(
            lax.slice_in_dim(block, block.shape[dim] - width, None, axis=dim), axis, forward
        )
        high = lax.ppermute(lax.slice_in_dim(block, 0, width, axis=dim), axis, backward)
        block = jnp.concatenate([low, block, high], axis=dim)
    return block


def zero_rim(values):
    widths = [(0, 0)] * (values.ndim - 3) + [(1, 1)] * 3
    return jnp.pad(values, widths)


def rim_cube(values):
    return extended(values, (("gx", 1), ("gy", 2), ("gz", 3)), 1)


def rim_slab(values):
    edged = extended(values, (("gy", 2), ("gz", 3)), 1)
    return jnp.pad(edged, ((0, 0), (1, 1), (0, 0), (0, 0)))


def across(padded, axis, offset):
    cells = padded.shape[-3:]
    lead = padded.ndim - 3
    starts = [0] * lead + [1, 1, 1]
    limits = list(padded.shape[:lead]) + [cells[0] - 1, cells[1] - 1, cells[2] - 1]
    starts[lead + axis] = offset
    limits[lead + axis] = cells[axis] - 2 + offset
    return lax.slice(padded, starts, limits)


def make_operator(faces, rim_fn):
    scale = lax.rsqrt(faces[0] + faces[1] + faces[2] + faces[3] + faces[4] + faces[5])

    def apply(values):
        padded = rim_fn(scale * values)
        beside_all = faces[0] * across(padded, 0, 0) + faces[1] * across(padded, 0, 2)
        beside_all = beside_all + faces[2] * across(padded, 1, 0) + faces[3] * across(padded, 1, 2)
        beside_all = beside_all + faces[4] * across(padded, 2, 0) + faces[5] * across(padded, 2, 2)
        return (1.0 + SPECTRAL_SHIFT) * values - scale * beside_all

    return apply


def chebyshev(apply, guess, target, lower_end, upper_end, degree):
    theta = 0.5 * (upper_end + lower_end)
    delta = 0.5 * (upper_end - lower_end)
    sigma = theta / delta
    ratio = 1.0 / sigma
    if guess is None:
        residual = target
    else:
        residual = target - apply(guess)
    update = residual / theta
    result = update if guess is None else guess + update
    for turn in range(degree - 1):
        residual = residual - apply(update)
        ratio_next = 1.0 / (2.0 * sigma - ratio)
        update = ratio_next * ratio * update + 2.0 * ratio_next / delta * residual
        ratio = ratio_next
        result = result + update
    return result


def restrict(values):
    lead = values.shape[:-3]
    cells = values.shape[-3:]
    depth = len(lead)
    grouped = values.reshape(lead + (cells[0] // 2, 2, cells[1] // 2, 2, cells[2] // 2, 2))
    return 0.125 * jnp.sum(grouped, axis=(depth + 1, depth + 3, depth + 5))


def prolong(values):
    lead = values.shape[:-3]
    cells = values.shape[-3:]
    expanded = values.reshape(lead + (cells[0], 1, cells[1], 1, cells[2], 1))
    expanded = jnp.broadcast_to(expanded, lead + (cells[0], 2, cells[1], 2, cells[2], 2))
    return expanded.reshape(lead + (2 * cells[0], 2 * cells[1], 2 * cells[2]))


def coarsen_faces(faces):
    cells = faces.shape[1:]
    halves = [cells[0] // 2, cells[1] // 2, cells[2] // 2]
    pieces = []
    for index in range(6):
        axis = index // 2
        picked = lax.slice_in_dim(faces[index], index % 2, cells[axis], stride=2, axis=axis)
        shape = [halves[0], 2, halves[1], 2, halves[2], 2]
        shape[2 * axis + 1] = 1
        pieces.append(0.25 * jnp.sum(picked.reshape(shape), axis=(1, 3, 5)))
    return jnp.stack(pieces)


def top_faces(affinity):
    padded = rim_cube(affinity)
    cells = affinity.shape[1:]
    offsets = (
        lax.axis_index("gx") * cells[0],
        lax.axis_index("gy") * cells[1],
        lax.axis_index("gz") * cells[2],
    )
    totals = (
        cells[0] * lax.axis_size("gx"),
        cells[1] * lax.axis_size("gy"),
        cells[2] * lax.axis_size("gz"),
    )
    pieces = []
    for axis in range(3):
        channel = affinity[axis]
        position = lax.broadcasted_iota(jnp.int32, cells, axis) + offsets[axis]
        below = across(padded[axis], axis, 0)
        above = across(padded[axis], axis, 2)
        pieces.append(jnp.where(position > 0, 0.5 * (below + channel), 0.0))
        pieces.append(jnp.where(position < totals[axis] - 1, 0.5 * (above + channel), 0.0))
    return jnp.stack(pieces)


def assemble(stack, counts):
    block = stack.shape[1:]
    grid = stack.reshape(counts + block)
    grid = grid.transpose(3, 0, 4, 1, 5, 2, 6)
    return grid.reshape(block[0], counts[0] * block[1], counts[1] * block[2], counts[2] * block[3])


def own_block(whole, starts, block):
    return lax.dynamic_slice(whole, (jnp.zeros((), jnp.int32),) + starts, (whole.shape[0],) + block)


def lower_cycle(target, faces):
    apply_fourth = make_operator(faces, zero_rim)
    result = chebyshev(apply_fourth, None, target, SMOOTH_LOWER, SMOOTH_UPPER, DEGREE)
    coarse_target = restrict(target - apply_fourth(result))
    apply_bottom = make_operator(coarsen_faces(faces), zero_rim)
    bottom = chebyshev(
        apply_bottom, None, coarse_target, SPECTRAL_SHIFT, SMOOTH_UPPER, COARSE_DEGREE
    )
    result = result + prolong(bottom)
    return chebyshev(apply_fourth, result, target, SMOOTH_LOWER, SMOOTH_UPPER, DEGREE)


def per_device(right_side, affinity):
    faces_top = top_faces(affinity)
    faces_second = coarsen_faces(faces_top)
    faces_third = coarsen_faces(faces_second)
    apply_top = make_operator(faces_top, rim_cube)
    apply_second = make_operator(faces_second, rim_cube)
    result_top = chebyshev(apply_top, None, right_side, SMOOTH_LOWER, SMOOTH_UPPER, DEGREE)
    target_second = restrict(right_side - apply_top(result_top))
    result_second = chebyshev(apply_second, None, target_second, SMOOTH_LOWER, SMOOTH_UPPER, DEGREE)
    target_third = restrict(target_second - apply_second(result_second))
    block = target_third.shape[1:]
    wide_target, wide_faces = (
        lax.all_gather(target_third, "gx", axis=1, tiled=True),
        lax.all_gather(faces_third, "gx", axis=1, tiled=True),
    )
    apply_third = make_operator(wide_faces, rim_slab)
    result_wide = chebyshev(apply_third, None, wide_target, SMOOTH_LOWER, SMOOTH_UPPER, DEGREE)
    target_fourth = restrict(wide_target - apply_third(result_wide))
    faces_fourth = coarsen_faces(wide_faces)
    gathered = (
        lax.all_gather(target_fourth[None], ("gy", "gz"), axis=0, tiled=True),
        lax.all_gather(faces_fourth[None], ("gy", "gz"), axis=0, tiled=True),
    )
    counts = (1, lax.axis_size("gy"), lax.axis_size("gz"))
    fourth = lower_cycle(assemble(gathered[0], counts), assemble(gathered[1], counts))
    piece = target_fourth.shape[1:]
    starts = (
        jnp.zeros((), jnp.int32),
        lax.axis_index("gy") * piece[1],
        lax.axis_index("gz") * piece[2],
    )
    result_wide = result_wide + prolong(own_block(fourth, starts, piece))
    result_wide = chebyshev(
        apply_third, result_wide, wide_target, SMOOTH_LOWER, SMOOTH_UPPER, DEGREE
    )
    result_third = lax.dynamic_slice_in_dim(
        result_wide, lax.axis_index("gx") * block[0], block[0], 1
    )
    result_second = result_second + prolong(result_third)
    result_second = chebyshev(
        apply_second, result_second, target_second, SMOOTH_LOWER, SMOOTH_UPPER, DEGREE
    )
    result_top = result_top + prolong(result_second)
    return chebyshev(apply_top, result_top, right_side, SMOOTH_LOWER, SMOOTH_UPPER, DEGREE)


def solution(mesh):
    in_specs = (P(None, "gx", "gy", "gz"), P(None, "gx", "gy", "gz"))
    out_specs = P(None, "gx", "gy", "gz")
    return jax.shard_map(
        per_device, mesh=mesh, in_specs=in_specs, out_specs=out_specs, check_vma=False
    )
```

profile of v0, /device:TPU:1, one launch (start us, length us, event | category | flops | bytes accessed | tf_op | source)
XLA Modules:
  0.0 1024.3 jit_solution(9413170714725753709)
XLA Ops:
  0.7 16.3 %collective-permute-start = (f32[3,1,8,128]{3,2,1,0:T(8,128)S(1)}, f32[3,1,8,128]{3,2,1,0:T(8,128)S(1)}, u32[]{:S(2)}, u32[]{:S(2)}) collective-permute-start(f32[3,1,8,128]{3,2,1,0:T(8,128)S(1)} %get-tuple-element.157), channel_id=1, source_target_pairs={{0,64},{64,128},{128,192},{192,256},{256,320},{320,384},{384,448},... | collective-permute-start | bytes 36872 | tf_op jit(solution)/shard_map/ppermute | solution.py:20
  19.2 10.9 %collective-permute-done.1 = f32[3,1,8,128]{3,2,1,0:T(8,128)S(1)} collective-permute-done((f32[3,1,8,128]{3,2,1,0:T(8,128)S(1)}, f32[3,1,8,128]{3,2,1,0:T(8,128)S(1)}, u32[]{:S(2)}, u32[]{:S(2)}) %collective-permute-start.1) | collective-permute-done | bytes 12320 | tf_op jit(solution)/shard_map/ppermute | solution.py:23
  63.1 11.8 %collective-permute-done.7 = f32[4,1,8,128]{3,2,1,0:T(8,128)S(1)} collective-permute-done((f32[4,1,8,128]{3,2,1,0:T(8,128)S(1)}, f32[4,1,8,128]{3,2,1,0:T(8,128)S(1)}, u32[]{:S(2)}, u32[]{:S(2)}) %collective-permute-start.7) | collective-permute-done | bytes 16416 | tf_op jit(solution)/shard_map/ppermute | solution.py:23
  79.0 55.3 %all_gather.13 = f32[6,16,2,32]{3,2,1,0:T(2,128)S(1)} all-gather(f32[6,2,2,32]{3,2,1,0:T(2,128)S(1)} %constant_dynamic-update-slice_fusion.12), channel_id=1, replica_groups=mesh['gx'=8,'gy'=8,'gz'=8] {'gx'}, dimensions={1}, use_global_device_ids=true | all-gather | bytes 27648 | tf_op jit(solution)/shard_map/all_gather | solution.py:174
  151.4 12.1 %collective-permute-start.12 = (f32[4,1,8,128]{3,2,1,0:T(8,128)S(1)}, f32[4,1,8,128]{3,2,1,0:T(8,128)S(1)}, u32[]{:S(2)}, u32[]{:S(2)}) collective-permute-start(f32[4,1,8,128]{3,2,1,0:T(8,128)S(1)} %get-tuple-element.144), channel_id=1, source_target_pairs={{0,64},{64,128},{128,192},{192,256},{256,320},{320,384},{384,448},... | collective-permute-start | bytes 49160 | tf_op jit(solution)/shard_map/ppermute | solution.py:20
  164.8 11.9 %collective-permute-done.13 = f32[4,1,8,128]{3,2,1,0:T(8,128)S(1)} collective-permute-done((f32[4,1,8,128]{3,2,1,0:T(8,128)S(1)}, f32[4,1,8,128]{3,2,1,0:T(8,128)S(1)}, u32[]{:S(2)}, u32[]{:S(2)}) %collective-permute-start.13) | collective-permute-done | bytes 16416 | tf_op jit(solution)/shard_map/ppermute | solution.py:23
  204.4 11.7 %collective-permute-done.19 = f32[4,1,8,128]{3,2,1,0:T(8,128)S(1)} collective-permute-done((f32[4,1,8,128]{3,2,1,0:T(8,128)S(1)}, f32[4,1,8,128]{3,2,1,0:T(8,128)S(1)}, u32[]{:S(2)}, u32[]{:S(2)}) %collective-permute-start.19) | collective-permute-done | bytes 16416 | tf_op jit(solution)/shard_map/ppermute | solution.py:23
  245.9 11.0 %collective-permute-start.24 = (f32[4,1,4,64]{3,2,1,0:T(4,128)S(1)}, f32[4,1,4,64]{3,2,1,0:T(4,128)S(1)}, u32[]{:S(2)}, u32[]{:S(2)}) collective-permute-start(f32[4,1,4,64]{3,2,1,0:T(4,128)S(1)} %get-tuple-element.216), channel_id=1, source_target_pairs={{0,64},{64,128},{128,192},{192,256},{256,320},{320,384},{384,448},... | collective-permute-start | bytes 12296 | tf_op jit(solution)/shard_map/ppermute | solution.py:20
  258.2 11.8 %collective-permute-done.25 = f32[4,1,4,64]{3,2,1,0:T(4,128)S(1)} collective-permute-done((f32[4,1,4,64]{3,2,1,0:T(4,128)S(1)}, f32[4,1,4,64]{3,2,1,0:T(4,128)S(1)}, u32[]{:S(2)}, u32[]{:S(2)}) %collective-permute-start.25) | collective-permute-done | bytes 4128 | tf_op jit(solution)/shard_map/ppermute | solution.py:23
  295.9 11.6 %collective-permute-done.31 = f32[4,1,4,64]{3,2,1,0:T(4,128)S(1)} collective-permute-done((f32[4,1,4,64]{3,2,1,0:T(4,128)S(1)}, f32[4,1,4,64]{3,2,1,0:T(4,128)S(1)}, u32[]{:S(2)}, u32[]{:S(2)}) %collective-permute-start.31) | collective-permute-done | bytes 4128 | tf_op jit(solution)/shard_map/ppermute | solution.py:23
  322.4 118.3 %all-gather.1 = f32[384,8,1,16]{3,1,2,0:T(8,128)S(1)} all-gather(f32[6,8,1,16]{3,1,2,0:T(8,128)S(1)} %constant_dynamic-update-slice_fusion.27), channel_id=3, replica_groups=mesh['gx'=8,'gy'=8,'gz'=8] {'gy','gz'}, dimensions={0}, use_global_device_ids=true | all-gather | bytes 199680 | tf_op jit(solution)/shard_map/all_gather | solution.py:182
  440.9 9.8 collective-permute-start.36
  452.2 11.7 %collective-permute-done.37 = f32[4,1,4,64]{3,2,1,0:T(4,128)S(1)} collective-permute-done((f32[4,1,4,64]{3,2,1,0:T(4,128)S(1)}, f32[4,1,4,64]{3,2,1,0:T(4,128)S(1)}, u32[]{:S(2)}, u32[]{:S(2)}) %collective-permute-start.37) | collective-permute-done | bytes 4128 | tf_op jit(solution)/shard_map/ppermute | solution.py:23
  478.8 57.0 %all_gather.12 = f32[4,16,2,32]{3,0,2,1:T(4,128)S(1)} all-gather(f32[4,2,2,32]{3,0,2,1:T(4,128)S(1)} %broadcast_multiply_fusion.26), channel_id=1, replica_groups=mesh['gx'=8,'gy'=8,'gz'=8] {'gx'}, dimensions={1}, use_global_device_ids=true | all-gather | bytes 18432 | tf_op jit(solution)/shard_map/all_gather | solution.py:173
  594.2 117.2 %all-gather = f32[256,8,16]{2,1,0:T(8,128)S(1)} all-gather(f32[4,8,16]{2,1,0:T(8,128)S(1)} %broadcast_multiply_fusion.24), channel_id=2, replica_groups=mesh['gx'=8,'gy'=8,'gz'=8] {'gy','gz'}, dimensions={0}, use_global_device_ids=true | all-gather | bytes 133120 | tf_op jit(solution)/shard_map/all_gather | solution.py:181
  782.4 11.8 %collective-permute-done.67 = f32[4,1,4,64]{3,2,1,0:T(4,128)S(1)} collective-permute-done((f32[4,1,4,64]{3,2,1,0:T(4,128)S(1)}, f32[4,1,4,64]{3,2,1,0:T(4,128)S(1)}, u32[]{:S(2)}, u32[]{:S(2)}) %collective-permute-start.67) | collective-permute-done | bytes 4128 | tf_op jit(solution)/shard_map/ppermute | solution.py:23
  811.0 10.8 %collective-permute-start.72 = (f32[4,1,4,64]{3,2,1,0:T(4,128)S(1)}, f32[4,1,4,64]{3,2,1,0:T(4,128)S(1)}, u32[]{:S(2)}, u32[]{:S(2)}) collective-permute-start(f32[4,1,4,64]{3,2,1,0:T(4,128)S(1)} %get-tuple-element.208), channel_id=1, source_target_pairs={{0,64},{64,128},{128,192},{192,256},{256,320},{320,384},{384,448},... | collective-permute-start | bytes 12296 | tf_op jit(solution)/shard_map/ppermute | solution.py:20
  823.1 11.8 %collective-permute-done.73 = f32[4,1,4,64]{3,2,1,0:T(4,128)S(1)} collective-permute-done((f32[4,1,4,64]{3,2,1,0:T(4,128)S(1)}, f32[4,1,4,64]{3,2,1,0:T(4,128)S(1)}, u32[]{:S(2)}, u32[]{:S(2)}) %collective-permute-start.73) | collective-permute-done | bytes 4128 | tf_op jit(solution)/shard_map/ppermute | solution.py:23
  856.0 11.8 %collective-permute-done.79 = f32[4,1,4,64]{3,2,1,0:T(4,128)S(1)} collective-permute-done((f32[4,1,4,64]{3,2,1,0:T(4,128)S(1)}, f32[4,1,4,64]{3,2,1,0:T(4,128)S(1)}, u32[]{:S(2)}, u32[]{:S(2)}) %collective-permute-start.79) | collective-permute-done | bytes 4128 | tf_op jit(solution)/shard_map/ppermute | solution.py:23
  891.9 11.5 %collective-permute-start.84 = (f32[4,1,8,128]{3,2,1,0:T(8,128)S(1)}, f32[4,1,8,128]{3,2,1,0:T(8,128)S(1)}, u32[]{:S(2)}, u32[]{:S(2)}) collective-permute-start(f32[4,1,8,128]{3,2,1,0:T(8,128)S(1)} %get-tuple-element.116), channel_id=1, source_target_pairs={{0,64},{64,128},{128,192},{192,256},{256,320},{320,384},{384,448},... | collective-permute-start | bytes 49160 | tf_op jit(solution)/shard_map/ppermute | solution.py:20
  904.7 12.0 %collective-permute-done.85 = f32[4,1,8,128]{3,2,1,0:T(8,128)S(1)} collective-permute-done((f32[4,1,8,128]{3,2,1,0:T(8,128)S(1)}, f32[4,1,8,128]{3,2,1,0:T(8,128)S(1)}, u32[]{:S(2)}, u32[]{:S(2)}) %collective-permute-start.85) | collective-permute-done | bytes 16416 | tf_op jit(solution)/shard_map/ppermute | solution.py:23
  944.4 11.9 %collective-permute-done.91 = f32[4,1,8,128]{3,2,1,0:T(8,128)S(1)} collective-permute-done((f32[4,1,8,128]{3,2,1,0:T(8,128)S(1)}, f32[4,1,8,128]{3,2,1,0:T(8,128)S(1)}, u32[]{:S(2)}, u32[]{:S(2)}) %collective-permute-start.91) | collective-permute-done | bytes 16416 | tf_op jit(solution)/shard_map/ppermute | solution.py:23
  977.4 12.0 %collective-permute-start.96 = (f32[4,1,8,128]{3,2,1,0:T(8,128)S(1)}, f32[4,1,8,128]{3,2,1,0:T(8,128)S(1)}, u32[]{:S(2)}, u32[]{:S(2)}) collective-permute-start(f32[4,1,8,128]{3,2,1,0:T(8,128)S(1)} %get-tuple-element.112), channel_id=1, source_target_pairs={{0,64},{64,128},{128,192},{192,256},{256,320},{320,384},{384,448},... | collective-permute-start | bytes 49160 | tf_op jit(solution)/shard_map/ppermute | solution.py:20
  990.8 11.9 %collective-permute-done.97 = f32[4,1,8,128]{3,2,1,0:T(8,128)S(1)} collective-permute-done((f32[4,1,8,128]{3,2,1,0:T(8,128)S(1)}, f32[4,1,8,128]{3,2,1,0:T(8,128)S(1)}, u32[]{:S(2)}, u32[]{:S(2)}) %collective-permute-start.97) | collective-permute-done | bytes 16416 | tf_op jit(solution)/shard_map/ppermute | solution.py:23
  (501 shorter events, 437.6 us)
Async XLA Ops:
  0.7 17.6 %collective-permute-start = (f32[3,1,8,128]{3,2,1,0:T(8,128)S(1)}, f32[3,1,8,128]{3,2,1,0:T(8,128)S(1)}, u32[]{:S(2)}, u32[]{:S(2)}) collective-permute-start(f32[3,1,8,128]{3,2,1,0:T(8,128)S(1)} %get-tuple-element.157), channel_id=1, source_target_pairs={{0,64},{64,128},{128,192},{192,256},{256,320},{320,384},{384,448},... | collective-permute-start | bytes 36872 | tf_op jit(solution)/shard_map/ppermute | solution.py:20
  17.0 13.2 %collective-permute-start.1 = (f32[3,1,8,128]{3,2,1,0:T(8,128)S(1)}, f32[3,1,8,128]{3,2,1,0:T(8,128)S(1)}, u32[]{:S(2)}, u32[]{:S(2)}) collective-permute-start(f32[3,1,8,128]{3,2,1,0:T(8,128)S(1)} %get-tuple-element.156), channel_id=1, source_target_pairs={{64,0},{128,64},{192,128},{256,192},{320,256},{384,320},{448,384},... | collective-permute-start | bytes 36872 | tf_op jit(solution)/shard_map/ppermute | solution.py:23
  61.6 13.3 %collective-permute-start.7 = (f32[4,1,8,128]{3,2,1,0:T(8,128)S(1)}, f32[4,1,8,128]{3,2,1,0:T(8,128)S(1)}, u32[]{:S(2)}, u32[]{:S(2)}) collective-permute-start(f32[4,1,8,128]{3,2,1,0:T(8,128)S(1)} %get-tuple-element.147), channel_id=1, source_target_pairs={{64,0},{128,64},{192,128},{256,192},{320,256},{384,320},{448,384},... | collective-permute-start | bytes 49160 | tf_op jit(solution)/shard_map/ppermute | solution.py:23
  74.9 59.4 %collective-permute-start.8 = (f32[4,10,1,128]{3,2,1,0:T(1,128)S(1)}, f32[4,10,1,128]{3,2,1,0:T(1,128)S(1)}, u32[]{:S(2)}, u32[]{:S(2)}) collective-permute-start(f32[4,10,1,128]{3,2,1,0:T(1,128)S(1)} %get-tuple-element.110), channel_id=1, source_target_pairs={{0,8},{8,16},{16,24},{24,32},{32,40},{40,48},{48,56},{1,9},{9,17},... | collective-permute-start | bytes 61448 | tf_op jit(solution)/shard_map/ppermute | solution.py:20
  77.7 56.6 %collective-permute-start.9 = (f32[4,10,1,128]{3,2,1,0:T(1,128)S(1)}, f32[4,10,1,128]{3,2,1,0:T(1,128)S(1)}, u32[]{:S(2)}, u32[]{:S(2)}) collective-permute-start(f32[4,10,1,128]{3,2,1,0:T(1,128)S(1)} %get-tuple-element.111), channel_id=1, source_target_pairs={{8,0},{16,8},{24,16},{32,24},{40,32},{48,40},{56,48},{9,1},{17,9},... | collective-permute-start | bytes 61448 | tf_op jit(solution)/shard_map/ppermute | solution.py:23
  134.6 12.1 %collective-permute-start.10 = (f32[4,10,10,1]{3,2,1,0:T(8,128)S(1)}, f32[4,10,10,1]{3,2,1,0:T(8,128)S(1)}, u32[]{:S(2)}, u32[]{:S(2)}) collective-permute-start(f32[4,10,10,1]{3,2,1,0:T(8,128)S(1)} %get-tuple-element.96), channel_id=1, source_target_pairs={{0,1},{1,2},{2,3},{3,4},{4,5},{5,6},{6,7},{8,9},{9,10},{10,11},{11... | collective-permute-start | bytes 4808 | tf_op jit(solution)/shard_map/ppermute | solution.py:20
  151.4 13.5 %collective-permute-start.12 = (f32[4,1,8,128]{3,2,1,0:T(8,128)S(1)}, f32[4,1,8,128]{3,2,1,0:T(8,128)S(1)}, u32[]{:S(2)}, u32[]{:S(2)}) collective-permute-start(f32[4,1,8,128]{3,2,1,0:T(8,128)S(1)} %get-tuple-element.144), channel_id=1, source_target_pairs={{0,64},{64,128},{128,192},{192,256},{256,320},{320,384},{384,448},... | collective-permute-start | bytes 49160 | tf_op jit(solution)/shard_map/ppermute | solution.py:20
  163.5 13.2 %collective-permute-start.13 = (f32[4,1,8,128]{3,2,1,0:T(8,128)S(1)}, f32[4,1,8,128]{3,2,1,0:T(8,128)S(1)}, u32[]{:S(2)}, u32[]{:S(2)}) collective-permute-start(f32[4,1,8,128]{3,2,1,0:T(8,128)S(1)} %get-tuple-element.145), channel_id=1, source_target_pairs={{64,0},{128,64},{192,128},{256,192},{320,256},{384,320},{448,384},... | collective-permute-start | bytes 49160 | tf_op jit(solution)/shard_map/ppermute | solution.py:23
  202.9 13.2 %collective-permute-start.19 = (f32[4,1,8,128]{3,2,1,0:T(8,128)S(1)}, f32[4,1,8,128]{3,2,1,0:T(8,128)S(1)}, u32[]{:S(2)}, u32[]{:S(2)}) collective-permute-start(f32[4,1,8,128]{3,2,1,0:T(8,128)S(1)} %get-tuple-element.143), channel_id=1, source_target_pairs={{64,0},{128,64},{192,128},{256,192},{320,256},{384,320},{448,384},... | collective-permute-start | bytes 49160 | tf_op jit(solution)/shard_map/ppermute | solution.py:23
  245.9 12.3 %collective-permute-start.24 = (f32[4,1,4,64]{3,2,1,0:T(4,128)S(1)}, f32[4,1,4,64]{3,2,1,0:T(4,128)S(1)}, u32[]{:S(2)}, u32[]{:S(2)}) collective-permute-start(f32[4,1,4,64]{3,2,1,0:T(4,128)S(1)} %get-tuple-element.216), channel_id=1, source_target_pairs={{0,64},{64,128},{128,192},{192,256},{256,320},{320,384},{384,448},... | collective-permute-start | bytes 12296 | tf_op jit(solution)/shard_map/ppermute | solution.py:20
  256.9 13.1 %collective-permute-start.25 = (f32[4,1,4,64]{3,2,1,0:T(4,128)S(1)}, f32[4,1,4,64]{3,2,1,0:T(4,128)S(1)}, u32[]{:S(2)}, u32[]{:S(2)}) collective-permute-start(f32[4,1,4,64]{3,2,1,0:T(4,128)S(1)} %get-tuple-element.217), channel_id=1, source_target_pairs={{64,0},{128,64},{192,128},{256,192},{320,256},{384,320},{448,384},... | collective-permute-start | bytes 12296 | tf_op jit(solution)/shard_map/ppermute | solution.py:23
  294.3 13.1 %collective-permute-start.31 = (f32[4,1,4,64]{3,2,1,0:T(4,128)S(1)}, f32[4,1,4,64]{3,2,1,0:T(4,128)S(1)}, u32[]{:S(2)}, u32[]{:S(2)}) collective-permute-start(f32[4,1,4,64]{3,2,1,0:T(4,128)S(1)} %get-tuple-element.215), channel_id=1, source_target_pairs={{64,0},{128,64},{192,128},{256,192},{320,256},{384,320},{448,384},... | collective-permute-start | bytes 12296 | tf_op jit(solution)/shard_map/ppermute | solution.py:23
  315.7 125.0 %collective-permute-start.34 = (f32[4,6,6,1]{3,0,2,1:T(4,128)S(1)}, f32[4,6,6,1]{3,0,2,1:T(4,128)S(1)}, u32[]{:S(2)}, u32[]{:S(2)}) collective-permute-start(f32[4,6,6,1]{3,0,2,1:T(4,128)S(1)} %get-tuple-element.176), channel_id=1, source_target_pairs={{0,1},{1,2},{2,3},{3,4},{4,5},{5,6},{6,7},{8,9},{9,10},{10,11},{11... | collective-permute-start | bytes 1736 | tf_op jit(solution)/shard_map/ppermute | solution.py:20
  320.5 120.2 %collective-permute-start.35 = (f32[4,6,6,1]{3,0,2,1:T(4,128)S(1)}, f32[4,6,6,1]{3,0,2,1:T(4,128)S(1)}, u32[]{:S(2)}, u32[]{:S(2)}) collective-permute-start(f32[4,6,6,1]{3,0,2,1:T(4,128)S(1)} %get-tuple-element.177), channel_id=1, source_target_pairs={{1,0},{2,1},{3,2},{4,3},{5,4},{6,5},{7,6},{9,8},{10,9},{11,10},{12... | collective-permute-start | bytes 1736 | tf_op jit(solution)/shard_map/ppermute | solution.py:23
  450.7 13.2 %collective-permute-start.37 = (f32[4,1,4,64]{3,2,1,0:T(4,128)S(1)}, f32[4,1,4,64]{3,2,1,0:T(4,128)S(1)}, u32[]{:S(2)}, u32[]{:S(2)}) collective-permute-start(f32[4,1,4,64]{3,2,1,0:T(4,128)S(1)} %get-tuple-element.213), channel_id=1, source_target_pairs={{64,0},{128,64},{192,128},{256,192},{320,256},{384,320},{448,384},... | collective-permute-start | bytes 12296 | tf_op jit(solution)/shard_map/ppermute | solution.py:23
  543.5 14.6 %collective-permute-start.44 = (f32[4,16,4,1]{3,1,2,0:T(8,128)S(1)}, f32[4,16,4,1]{3,1,2,0:T(8,128)S(1)}, u32[]{:S(2)}, u32[]{:S(2)}) collective-permute-start(f32[4,16,4,1]{3,1,2,0:T(8,128)S(1)} %get-tuple-element.140), channel_id=1, source_target_pairs={{0,1},{1,2},{2,3},{3,4},{4,5},{5,6},{6,7},{8,9},{9,10},{10,11},{11... | collective-permute-start | bytes 3080 | tf_op jit(solution)/shard_map/ppermute | solution.py:20
  781.1 13.1 %collective-permute-start.67 = (f32[4,1,4,64]{3,2,1,0:T(4,128)S(1)}, f32[4,1,4,64]{3,2,1,0:T(4,128)S(1)}, u32[]{:S(2)}, u32[]{:S(2)}) collective-permute-start(f32[4,1,4,64]{3,2,1,0:T(4,128)S(1)} %get-tuple-element.211), channel_id=1, source_target_pairs={{64,0},{128,64},{192,128},{256,192},{320,256},{384,320},{448,384},... | collective-permute-start | bytes 12296 | tf_op jit(solution)/shard_map/ppermute | solution.py:23
  821.8 13.1 %collective-permute-start.73 = (f32[4,1,4,64]{3,2,1,0:T(4,128)S(1)}, f32[4,1,4,64]{3,2,1,0:T(4,128)S(1)}, u32[]{:S(2)}, u32[]{:S(2)}) collective-permute-start(f32[4,1,4,64]{3,2,1,0:T(4,128)S(1)} %get-tuple-element.209), channel_id=1, source_target_pairs={{64,0},{128,64},{192,128},{256,192},{320,256},{384,320},{448,384},... | collective-permute-start | bytes 12296 | tf_op jit(solution)/shard_map/ppermute | solution.py:23
  854.7 13.1 %collective-permute-start.79 = (f32[4,1,4,64]{3,2,1,0:T(4,128)S(1)}, f32[4,1,4,64]{3,2,1,0:T(4,128)S(1)}, u32[]{:S(2)}, u32[]{:S(2)}) collective-permute-start(f32[4,1,4,64]{3,2,1,0:T(4,128)S(1)} %get-tuple-element.207), channel_id=1, source_target_pairs={{64,0},{128,64},{192,128},{256,192},{320,256},{384,320},{448,384},... | collective-permute-start | bytes 12296 | tf_op jit(solution)/shard_map/ppermute | solution.py:23
  891.9 12.8 %collective-permute-start.84 = (f32[4,1,8,128]{3,2,1,0:T(8,128)S(1)}, f32[4,1,8,128]{3,2,1,0:T(8,128)S(1)}, u32[]{:S(2)}, u32[]{:S(2)}) collective-permute-start(f32[4,1,8,128]{3,2,1,0:T(8,128)S(1)} %get-tuple-element.116), channel_id=1, source_target_pairs={{0,64},{64,128},{128,192},{192,256},{256,320},{320,384},{384,448},... | collective-permute-start | bytes 49160 | tf_op jit(solution)/shard_map/ppermute | solution.py:20
  903.4 13.3 %collective-permute-start.85 = (f32[4,1,8,128]{3,2,1,0:T(8,128)S(1)}, f32[4,1,8,128]{3,2,1,0:T(8,128)S(1)}, u32[]{:S(2)}, u32[]{:S(2)}) collective-permute-start(f32[4,1,8,128]{3,2,1,0:T(8,128)S(1)} %get-tuple-element.117), channel_id=1, source_target_pairs={{64,0},{128,64},{192,128},{256,192},{320,256},{384,320},{448,384},... | collective-permute-start | bytes 49160 | tf_op jit(solution)/shard_map/ppermute | solution.py:23
  943.0 13.2 %collective-permute-start.91 = (f32[4,1,8,128]{3,2,1,0:T(8,128)S(1)}, f32[4,1,8,128]{3,2,1,0:T(8,128)S(1)}, u32[]{:S(2)}, u32[]{:S(2)}) collective-permute-start(f32[4,1,8,128]{3,2,1,0:T(8,128)S(1)} %get-tuple-element.115), channel_id=1, source_target_pairs={{64,0},{128,64},{192,128},{256,192},{320,256},{384,320},{448,384},... | collective-permute-start | bytes 49160 | tf_op jit(solution)/shard_map/ppermute | solution.py:23
  977.4 13.3 %collective-permute-start.96 = (f32[4,1,8,128]{3,2,1,0:T(8,128)S(1)}, f32[4,1,8,128]{3,2,1,0:T(8,128)S(1)}, u32[]{:S(2)}, u32[]{:S(2)}) collective-permute-start(f32[4,1,8,128]{3,2,1,0:T(8,128)S(1)} %get-tuple-element.112), channel_id=1, source_target_pairs={{0,64},{64,128},{128,192},{192,256},{256,320},{320,384},{384,448},... | collective-permute-start | bytes 49160 | tf_op jit(solution)/shard_map/ppermute | solution.py:20
  989.5 13.2 %collective-permute-start.97 = (f32[4,1,8,128]{3,2,1,0:T(8,128)S(1)}, f32[4,1,8,128]{3,2,1,0:T(8,128)S(1)}, u32[]{:S(2)}, u32[]{:S(2)}) collective-permute-start(f32[4,1,8,128]{3,2,1,0:T(8,128)S(1)} %get-tuple-element.113), channel_id=1, source_target_pairs={{64,0},{128,64},{192,128},{256,192},{320,256},{384,320},{448,384},... | collective-permute-start | bytes 49160 | tf_op jit(solution)/shard_map/ppermute | solution.py:23
  (79 other events, 447.9 us)
where the time goes:
time: 1040 us; the launch traced here: 1020 us
  blocking collectives  348 us (33%)
  starting transfers between devices  320 us (31%)
  waiting for transfers between devices  293 us (28%)
  local copies, waits for them, and re-layouts  35.8 us (3%)
  other arithmetic  25.3 us (2%)
    ppermute x51, waiting for transfers between devices, extended(): lax.ppermute(lax.slice_in_dim(block, 0, width, axis=dim), axis, backward)  279 us
    ppermute x51, starting transfers between devices, extended(): lax.ppermute(lax.slice_in_dim(block, block.shape[dim] - width, None, axis...  239 us
    all_gather x1, blocking collectives, per_device(): lax.all_gather(faces_fourth[None], ('gy', 'gz'), axis=0, tiled=True)  118 us
    all_gather x1, blocking collectives, per_device(): lax.all_gather(target_fourth[None], ('gy', 'gz'), axis=0, tiled=True)  117 us
    ppermute x51, starting transfers between devices, extended(): lax.ppermute(lax.slice_in_dim(block, 0, width, axis=dim), axis, backward)  80.8 us
    all_gather x1, blocking collectives, per_device(): lax.all_gather(target_third, 'gx', axis=1, tiled=True)  57 us
    all_gather x1, blocking collectives, per_device(): lax.all_gather(faces_third, 'gx', axis=1, tiled=True)  55.3 us
  transfers between devices with their start and end apart: 102, of which 56 were waited for; matrix products, arithmetic and copies ran while one was open for 1% of the time, Pallas kernels for 0%

commit v1 on v0

v1 whole, which is shorter than its diff:
```python
import functools

import jax
import jax.numpy as jnp
from jax import lax
from jax.experimental import pallas as pl
from jax.experimental.pallas import tpu as pltpu
from jax.sharding import PartitionSpec as P

MESH = pl.DeviceIdType.MESH
HIGHEST = lax.Precision.HIGHEST
F32 = jnp.float32

DEGREE = 3
COARSE_DEGREE = 8
SHIFT = 0.02
SMOOTH_LOWER = 0.5
UPPER = 2.0 + SHIFT


def cheb_coefs(a, b, m):
    theta, delta = 0.5 * (b + a), 0.5 * (b - a)
    sigma = theta / delta
    rho = 1.0 / sigma
    steps = []
    for _ in range(m - 1):
        nxt = 1.0 / (2.0 * sigma - rho)
        steps.append((nxt * rho, 2.0 * nxt / delta))
        rho = nxt
    return 1.0 / theta, steps


SMOOTH = cheb_coefs(SMOOTH_LOWER, UPPER, DEGREE)
SOLVE = cheb_coefs(SHIFT, UPPER, COARSE_DEGREE)


def iota(dim, shape=(1, 8, 128)):
    return lax.broadcasted_iota(jnp.int32, shape, dim)


def roll(x, shift, axis):
    shift = shift % x.shape[axis]
    return x if shift == 0 else pltpu.roll(x, shift, axis)


def both(x, k, axis):
    bit = (iota(axis, (1,) + x.shape[1:]) // k) % 2
    return x + jnp.where(bit == 0, roll(x, -k, axis), roll(x, k, axis))


def pick(x, k, axis, upper):
    bit = (iota(axis, (1,) + x.shape[1:]) // k) % 2
    if upper:
        return jnp.where(bit == 1, x, roll(x, -k, axis))
    return jnp.where(bit == 0, x, roll(x, k, axis))


def slots(ref, start, count, rows=16):
    if not isinstance(start, int):
        start = pl.multiple_of(start * rows, rows)
    else:
        start = start * rows
    return ref[pl.ds(start, count * rows), :].reshape(count, rows, 128)


def put(ref, start, value):
    count, rows = value.shape[:2]
    if not isinstance(start, int):
        start = pl.multiple_of(start * rows, rows)
    else:
        start = start * rows
    ref[pl.ds(start, count * rows), :] = value.reshape(count * rows, 128)


def loop(count, body):
    def run(i, carry):
        body(i)
        return carry

    lax.fori_loop(0, count, run, 0)


class Level:
    def __init__(self, z, rows, sy, sx, mode, refs):
        self.z, self.rows, self.sy, self.sx, self.mode = z, rows, sy, sx, mode
        self.ch = 128 // rows
        self.turns = z // self.ch
        (self.coef, self.scale, self.f, self.r, self.d, self.x, self.wa, self.wb, self.up, self.low) = refs

    def get(self, ref, i, offset=0):
        return slots(ref, i * self.ch + offset, self.ch, self.rows)

    def put(self, ref, i, value, offset=0):
        put(ref, i * self.ch + offset, value)


LEVELS = ((72, 16, 1, 1, 0), (72, 16, 1, 1, 0), (48, 16, 1, 2, 0), (32, 8, 1, 4, 1), (32, 8, 2, 8, 2))


def level_shapes(z, rows):
    n = z * rows
    pad = (z + 2) * rows
    return [pltpu.VMEM((6 * n, 128), F32)] + [pltpu.VMEM((n, 128), F32)] * 5 + [pltpu.VMEM((pad, 128), F32)] * 2 + [
        pltpu.VMEM((n, 128), F32)] * 2


def neighbours(lv, w_ref, i):
    w, before, after = lv.get(w_ref, i, 1), lv.get(w_ref, i, 0), lv.get(w_ref, i, 2)
    xd, xu = roll(w, lv.sx, 2), roll(w, -lv.sx, 2)
    yd, yu = roll(w, lv.sy, 1), roll(w, -lv.sy, 1)
    if lv.mode == 0:
        zd, zu = before, after
    else:
        s = lv.mode
        t = iota(2) % 4
        zu = jnp.where(t < 4 - s, roll(w, -s, 2), roll(after, 4 - s, 2))
        zd = jnp.where(t >= s, roll(w, s, 2), roll(before, s - 4, 2))
    return w, xd, xu, yd, yu, zd, zu


def apply_at(lv, w_ref, i):
    _, *near = neighbours(lv, w_ref, i)
    total = None
    for k, value in enumerate(near):
        term = slots(lv.coef, k * lv.z + i * lv.ch, lv.ch, lv.rows) * value
        total = term if total is None else total + term
    return total


def init_down(lv, over_theta):
    def body(i):
        f = lv.get(lv.f, i)
        d = f * over_theta
        lv.put(lv.r, i, f)
        lv.put(lv.d, i, d)
        lv.put(lv.x, i, d)
        lv.put(lv.wa, i, lv.get(lv.scale, i) * d, 1)

    loop(lv.turns, body)


def init_up(lv, coarse_at):
    def body(i):
        d = coarse_at(i)
        lv.put(lv.d, i, d)
        lv.put(lv.x, i, lv.get(lv.x, i) + d)
        lv.put(lv.wa, i, lv.get(lv.scale, i) * d, 1)

    loop(lv.turns, body)


def step(lv, w_ref, w_next, alpha=None, beta=None, last=False):
    def body(i):
        d = lv.get(lv.d, i)
        r = lv.get(lv.r, i) - ((1.0 + SHIFT) * d - apply_at(lv, w_ref, i))
        if not last:
            lv.put(lv.r, i, r)
        if beta is None:
            return
        d = beta * r if alpha is None else alpha * d + beta * r
        lv.put(lv.x, i, lv.get(lv.x, i) + d)
        if not last:
            lv.put(lv.d, i, d)
            lv.put(w_next, i, lv.get(lv.scale, i) * d, 1)

    loop(lv.turns, body)


def make_coefs(lv, group):
    g = (iota(2, (1, lv.rows, 128)) // group) % 4

    def spread(value, k):
        out = value
        for to in range(4):
            if to != k:
                out = jnp.where(g == to, roll(value, group * (to - k), 2), out)
        return out

    def body(i):
        low, up = lv.get(lv.low, i), lv.get(lv.up, i)
        faces = []
        for k in range(3):
            faces += [spread(low, k), spread(up, k)]
        total = faces[0] + faces[1] + faces[2] + faces[3] + faces[4] + faces[5]
        scale = jnp.where(total > 0.0, lax.rsqrt(total), 0.0)
        lv.put(lv.scale, i, scale)
        for k in range(6):
            put(lv.coef, k * lv.z + i * lv.ch, scale * faces[k])

    loop(lv.turns, body)


def own_pairs(ref, i):
    v = slots(ref, 4 + 32 * i, 32)[:, :8].reshape(16, 2, 8, 128)
    return v[:, 0], v[:, 1]


def coarse_faces(first, second, group, upper, ky, kx):
    g = (iota(2) // group) % 4
    v = jnp.where(g == 2, second if upper else first, first + second)
    v = jnp.where(g == 1, pick(v, ky, 1, upper), both(v, ky, 1))
    if kx is not None:
        v = jnp.where(g == 0, pick(v, kx, 2, upper), both(v, kx, 2))
    return v


def kernel(nx, ny, nz, f_hbm, a_hbm, out_ref, *scratch):
    refs = list(scratch)

    def take(count):
        got = refs[:count]
        del refs[:count]
        return got

    levels = [Level(*shape, take(10)) for shape in LEVELS]
    (fext, aext, ys, yr, zs, zr, tb, tmp, xg1, xgf, rxs, rxr, pz1, pzf, yg1, ygf, eb2, eb1, eb0) = take(19)
    (local_sem, strip_send, strip_recv, ex_send, ex_recv, xg_send, xg_recv, rx_send, rx_recv,
     pz_send, pz_recv, yg_send, yg_recv, zg_send, zg_recv) = take(15)
    l0, l1, l2, l3, l4 = levels

    b, j, k = lax.axis_index("gx"), lax.axis_index("gy"), lax.axis_index("gz")
    sub, lane, lane16 = iota(1), iota(2), iota(2, (1, 16, 128))
    lane2 = lax.broadcasted_iota(jnp.int32, (1, 128), 1)

    def remote(src, dst, send, recv, **to):
        return pltpu.make_async_remote_copy(
            src_ref=src, dst_ref=dst, send_sem=send, recv_sem=recv, device_id=to, device_id_type=MESH)

    own_f = pltpu.make_async_copy(f_hbm, fext.at[:, pl.ds(4, 8)], local_sem.at[0])
    own_a = pltpu.make_async_copy(a_hbm, aext.at[pl.ds(0, 3), pl.ds(4, 8)], local_sem.at[1])
    own_a.start()
    own_f.start()
    zr[...] = jnp.zeros_like(zr)

    barrier = pltpu.get_barrier_semaphore()
    partners = [{"gx": lax.rem(b + t, 8)} for t in (1, 2, 4, 6, 7)]
    partners += [{"gy": lax.rem(j + t, 8)} for t in range(1, 8)]
    partners += [{"gz": lax.rem(k + t, 8)} for t in range(1, 8)]
    partners += [{"gy": lax.rem(j + t, 8), "gz": lax.rem(k + u, 8)} for t in (1, 7) for u in (1, 7)]
    for to in partners:
        pl.semaphore_signal(barrier, inc=1, device_id=to, device_id_type=MESH)

    fext[:, 0] = jnp.zeros((4, 8, 128), F32)
    fext[:, 15] = jnp.zeros((4, 8, 128), F32)
    aext[3] = jnp.zeros((16, 8, 128), F32)
    for ref in (l0.f, l0.wa, l1.f, l1.up, l1.low, eb1):
        ref[...] = jnp.zeros_like(ref)
    for lv in levels:
        for w in (lv.wa, lv.wb):
            w[pl.ds(0, lv.rows), :] = jnp.zeros((lv.rows, 128), F32)
            w[pl.ds((lv.z + 1) * lv.rows, lv.rows), :] = jnp.zeros((lv.rows, 128), F32)
    pl.semaphore_wait(barrier, len(partners))

    b_up, b_down = lax.rem(b + 1, 8), lax.rem(b + 7, 8)
    strips = [
        remote(a_hbm.at[:, pl.ds(4, 4)], aext.at[pl.ds(0, 3), pl.ds(0, 4)],
               strip_send.at[0], strip_recv.at[0], gx=b_up),
        remote(a_hbm.at[:, pl.ds(0, 4)], aext.at[pl.ds(0, 3), pl.ds(12, 4)],
               strip_send.at[1], strip_recv.at[1], gx=b_down),
        remote(f_hbm.at[:, pl.ds(5, 3)], fext.at[:, pl.ds(1, 3)],
               strip_send.at[2], strip_recv.at[2], gx=b_up),
        remote(f_hbm.at[:, pl.ds(0, 3)], fext.at[:, pl.ds(12, 3)],
               strip_send.at[3], strip_recv.at[3], gx=b_down),
    ]
    for copy in strips:
        copy.start()

    class Wide:
        def __init__(self, n, block, ref, base, h):
            self.n, self.block, self.ref, self.base, self.h = n, block, ref, base, h
            rows, part = pl.ds(0, h), pl.ds(0, h * 8)
            j_up, j_down = jnp.minimum(j + 1, 7), jnp.maximum(j - 1, 0)
            k_to = (lax.rem(k + 1, 8), lax.rem(k + 7, 8))

            def make(src, dst, index, **to):
                return remote(src, dst, ex_send.at[n, index], ex_recv.at[n, index], **to)

            self.up = [make(ys.at[n, 0, rows], yr.at[n, 0, rows], 0, gy=j_up)]
            self.down = [make(ys.at[n, 1, rows], yr.at[n, 1, rows], 1, gy=j_down)]
            self.flat = []
            for dz in range(2):
                self.flat.append(make(zs.at[n, dz, part], zr.at[n, dz, 0, part], 2 + dz, gz=k_to[dz]))
                self.up.append(make(zs.at[n, dz, part], zr.at[n, dz, 1, part], 4 + dz, gy=j_up, gz=k_to[dz]))
                self.down.append(make(zs.at[n, dz, part], zr.at[n, dz, 2, part], 6 + dz, gy=j_down, gz=k_to[dz]))

        def start(self):
            n, block, ref, base, h = self.n, self.block, self.ref, self.base, self.h
            for i in range(h):
                ys[n, 0, i] = ref[pl.ds((base + 4) * 16 + block - h + i, 64, stride=16), :]
                ys[n, 1, i] = ref[pl.ds((base + 4) * 16 + i, 64, stride=16), :]
                zs[n, 0, pl.ds(i * 8, 8), :] = ref[pl.ds((base + 68 - h + i) * 16, 8), :]
                zs[n, 1, pl.ds(i * 8, 8), :] = ref[pl.ds((base + 4 + i) * 16, 8), :]

            @pl.when(j < 7)
            def _():
                for copy in self.up:
                    copy.start()

            @pl.when(j > 0)
            def _():
                for copy in self.down:
                    copy.start()

            for copy in self.flat:
                copy.start()

        def finish(self):
            n, block, ref, base, h = self.n, self.block, self.ref, self.base, self.h

            @pl.when(j > 0)
            def _():
                for copy in self.up:
                    copy.wait_recv()
                for i in range(h):
                    ref[pl.ds((base + 4) * 16 + 16 - h + i, 64, stride=16), :] = yr[n, 0, i]

            @pl.when(j < 7)
            def _():
                for copy in self.down:
                    copy.wait_recv()
                for i in range(h):
                    ref[pl.ds((base + 4) * 16 + block + i, 64, stride=16), :] = yr[n, 1, i]

            for copy in self.flat:
                copy.wait_recv()
            for dz in range(2):
                here, low, high = (zr[n, dz, m, pl.ds(0, h * 8), :].reshape(h, 8, 128) for m in range(3))
                if block == 8:
                    pair = [here, jnp.where(sub < 4, high, low)]
                else:
                    pair = [jnp.where(sub < 4, here, roll(high, 4, 1)), roll(low, 4, 1)]
                v = jnp.concatenate(pair, axis=1)
                if block == 8:
                    if dz == 0:
                        v = roll(jnp.where(lane16 < 64, slots(ref, base + 68 - h, h), v), 64, 2)
                    else:
                        v = roll(jnp.where(lane16 < 64, v, slots(ref, base + 4, h)), 64, 2)
                put(ref, base + (4 - h if dz == 0 else 68), v)

            @pl.when(j < 7)
            def _():
                for copy in self.up:
                    copy.wait_send()

            @pl.when(j > 0)
            def _():
                for copy in self.down:
                    copy.wait_send()

            for copy in self.flat:
                copy.wait_send()

    half_lane = lax.broadcasted_iota(jnp.int32, (64, 128), 1) < 64

    def to_tiles(src, dst, base):
        for y in range(0, 8, 2):
            rows = [src[pl.ds(y + d, 64, stride=8), :] for d in range(2)]
            turned = jnp.concatenate(rows, axis=0).T
            low, high = turned[:64], turned[64:]
            first = (base + 4) * 16 + y
            dst[pl.ds(first, 64, stride=16), :] = jnp.where(half_lane, low, pltpu.roll(high, 64, 1))
            dst[pl.ds(first + 1, 64, stride=16), :] = jnp.where(half_lane, pltpu.roll(low, 64, 1), high)

    fext_rows, aext_rows = fext.reshape(512, 128), aext.reshape(512, 128)

    def x_gather(xg, n):
        first = remote(xg.at[b], xg.at[b], xg_send.at[n, 0], xg_recv.at[n, 0], gx=b + 1 - 2 * lax.rem(b, 2))
        pair = pl.ds((b // 2) * 2, 2)
        second = [remote(xg.at[pair], xg.at[pair], xg_send.at[n, t], xg_recv.at[n, t], gx=lax.rem(b + 2 * t, 8))
                  for t in range(1, 4)]
        return first, second

    def x_pack(weight, xg, first, upper=None):
        source = lax.broadcasted_iota(jnp.int32, (128, 256), 0)
        target = lax.broadcasted_iota(jnp.int32, (128, 256), 1)
        slot, inner = source % 16, (target % 128) % 32
        hit = (source // 64 == target // 128) & ((source % 64) // 16 == (target % 128) // 32) & (inner < 4)
        pair = (slot // 2 == inner + 2) & hit
        if upper is not None:
            pair = pair & (((source % 64) // 16 != 0) | (slot % 2 == (1 if upper else 0)))
        matrix = jnp.where(pair, weight, 0.0).astype(F32)
        moved = jnp.dot(tb[...], matrix, precision=HIGHEST, preferred_element_type=F32)
        parts = [moved[:, :128].reshape(32, 8, 128), moved[:, 128:].reshape(32, 8, 128)]
        total = None
        for g in range(8):
            part = roll(parts[g // 4][(g % 4) * 8:(g % 4) * 8 + 8], 4 * g, 2)
            total = part if total is None else total + part
        packed = jnp.where(sub % 2 == 0, total[:4], total[4:])
        xg[b, pl.ds(first * 8, 32), :] = packed.reshape(32, 128)

    def x_unpack(xg, first, dst):
        g = (lane // 4) % 8
        for q in range(4):
            for odd in range(2):
                v = []
                for n in range(8):
                    tile = xg[n, pl.ds((first + q) * 8, 8), :].reshape(1, 8, 128)
                    v.append(jnp.where(sub % 2 == 1, tile, roll(tile, -1, 1)) if odd
                             else jnp.where(sub % 2 == 0, tile, roll(tile, 1, 1)))
                for s in (1, 2, 4):
                    high = (g // s) % 2 == 1
                    for n in range(8):
                        if n & s == 0:
                            lo, hi = v[n], v[n + s]
                            v[n] = jnp.where(high, roll(hi, 4 * s, 2), lo)
                            v[n + s] = jnp.where(high, hi, roll(lo, -4 * s, 2))
                for n in range(8):
                    put(tmp, n * 8 + 4 * odd + q, v[n])
        for i in range(4):
            dst[pl.ds(64 + i, 64, stride=16), :] = tmp[pl.ds(2 * i, 64, stride=8), :]

    own_a.wait()
    strips[0].wait_recv()
    strips[1].wait_recv()
    to_tiles(aext_rows, l0.wa, 1)
    edges = Wide(0, 8, l0.wa, 1, 4)
    edges.start()
    edges.finish()
    group0 = (lane16 // 16) % 4
    row16 = iota(1, (1, 16, 128))
    x_at = 8 * b + lane16 % 16 - 4
    y_at = 8 * j + jnp.where(row16 < 12, row16, row16 - 16)

    def face_body(i):
        a, xd, xu, yd, yu, zd, zu = neighbours(l0, l0.wa, i)
        z_at = 128 * k + 64 * (iota(2, a.shape) // 64) + i * l0.ch - 4 + iota(0, a.shape)
        side_up = jnp.where(group0 == 0, xu, jnp.where(group0 == 1, yu, zu))
        side_low = jnp.where(group0 == 0, xd, jnp.where(group0 == 1, yd, zd))
        where = jnp.where(group0 == 0, x_at, jnp.where(group0 == 1, y_at, z_at))
        end = jnp.where(group0 == 0, nx - 1, jnp.where(group0 == 1, ny - 1, nz - 1))
        l0.put(l0.up, i, jnp.where(where == end, 0.0, 0.5 * (a + side_up)))
        l0.put(l0.low, i, jnp.where(where == 0, 0.0, 0.5 * (a + side_low)))

    loop(l0.turns, face_body)

    for upper, ref in ((True, l0.up), (False, l0.low)):
        def body(i, ref=ref, upper=upper):
            put(tb, i * 16, coarse_faces(*own_pairs(ref, i), 16, upper, 1, None))

        loop(2, body)
        x_pack(0.25, xgf, 0 if upper else 4, upper)
    faces_first, faces_second = x_gather(xgf, 1)
    faces_first.start()
    make_coefs(l0, 16)

    own_f.wait()
    strips[2].wait_recv()
    strips[3].wait_recv()
    to_tiles(fext_rows, l0.f, 0)
    edges = Wide(1, 8, l0.f, 0, 3)
    edges.start()
    faces_first.wait_recv()
    for copy in faces_second:
        copy.start()
    edges.finish()

    over_theta, ((a1, b1), (a2, b2)) = SMOOTH

    def downward(lv):
        init_down(lv, over_theta)
        step(lv, lv.wa, lv.wb, a1, b1)
        step(lv, lv.wb, lv.wa, a2, b2)
        step(lv, lv.wa, None)

    def upward(lv, coarse_at):
        init_up(lv, coarse_at)
        step(lv, lv.wa, lv.wb, None, over_theta)
        step(lv, lv.wb, lv.wa, a1, b1)
        step(lv, lv.wa, None, a2, b2, last=True)

    downward(l0)

    def body(i):
        first, second = own_pairs(l0.r, i)
        put(tb, i * 16, both(first + second, 1, 1))

    loop(2, body)
    x_pack(0.125, xg1, 0)
    right_first, right_second = x_gather(xg1, 0)
    right_first.start()

    slot = lane % 16
    for side, first in ((0, 10), (1, 4)):
        packed = jnp.zeros((8, 8, 128), F32)
        for g in range(8):
            v = slots(l0.r, 4 + 8 * g, 8)[:, :8]
            packed = jnp.where(slot // 2 == g, roll(v, 2 * g - first, 2), packed)
        rxs[side] = packed.reshape(64, 128)
    rx = [remote(rxs.at[0], rxr.at[0], rx_send.at[0], rx_recv.at[0], gx=b_up),
          remote(rxs.at[1], rxr.at[1], rx_send.at[1], rx_recv.at[1], gx=b_down)]
    for copy in rx:
        copy.start()

    for copy in faces_second:
        copy.wait_recv()
    x_unpack(xgf, 0, l1.up)
    x_unpack(xgf, 4, l1.low)
    edges_up, edges_low = Wide(2, 4, l1.up, 0, 3), Wide(3, 4, l1.low, 0, 3)
    edges_up.start()
    edges_low.start()

    def second_pack(pz, first):
        v = jnp.where(lane2 % 2 == 0, tb[pl.ds(0, 32, stride=8), :], tb[pl.ds(2, 32, stride=8), :])
        pz[pl.ds(first + 8, 32), :] = v

    def second_edges(pz, first, n):
        up, down = pl.ds(first + 32, 8), pl.ds(first + 8, 8)
        return [remote(pz.at[up], pz.at[pl.ds(first, 8)], pz_send.at[n, 0], pz_recv.at[n, 0], gz=lax.rem(k + 1, 8)),
                remote(pz.at[down], pz.at[pl.ds(first + 40, 8)], pz_send.at[n, 1], pz_recv.at[n, 1],
                       gz=lax.rem(k + 7, 8))]

    def y_gather(pz, yg, n):
        return [remote(pz, yg.at[j], yg_send.at[n, t], yg_recv.at[n, t], gy=lax.rem(j + t, 8)) for t in range(1, 8)]

    def second_unpack(yg, first, dst):
        for n in range(8):
            v = yg[n, pl.ds(first, 48), :]
            dst[pl.ds(2 * n, 48, stride=16), :] = jnp.where(lane2 % 2 == 0, v, roll(v, 1, 1))
            dst[pl.ds(2 * n + 1, 48, stride=16), :] = jnp.where(lane2 % 2 == 1, v, roll(v, -1, 1))

    for upper, ref in ((True, l1.up), (False, l1.low)):
        def body(i, ref=ref, upper=upper):
            put(tb, i * 16, 0.25 * coarse_faces(*own_pairs(ref, i), 32, upper, 1, 1))

        loop(2, body)
        second_pack(pzf, 0 if upper else 48)
    faces_z = second_edges(pzf, 0, 0) + second_edges(pzf, 48, 1)
    for copy in faces_z:
        copy.start()
    edges_up.finish()
    edges_low.finish()
    make_coefs(l1, 32)
    for copy in faces_z:
        copy.wait_recv()
    ygf[j] = pzf[...]
    faces_y = y_gather(pzf, ygf, 0)
    for copy in faces_y:
        copy.start()

    right_first.wait_recv()
    for copy in right_second:
        copy.start()
    for copy in faces_y:
        copy.wait_recv()
    second_unpack(ygf, 0, l2.up)
    second_unpack(ygf, 48, l2.low)
    for copy in right_second:
        copy.wait_recv()
    x_unpack(xg1, 0, l1.f)
    edges = Wide(4, 4, l1.f, 0, 3)
    edges.start()
    make_coefs(l2, 32)
    edges.finish()
    downward(l1)

    def body(i):
        first, second = own_pairs(l1.r, i)
        put(tb, i * 16, 0.125 * both(both(first + second, 1, 1), 1, 2))

    loop(2, body)
    second_pack(pz1, 0)
    right_z = second_edges(pz1, 0, 2)
    for copy in right_z:
        copy.start()
    edges1 = Wide(5, 4, l1.r, 0, 2)
    edges1.start()

    t = lane % 4

    def third(ref, upper=None):
        even, odd = (ref[pl.ds(128 + d, 256, stride=2), :].reshape(16, 2, 8, 128) for d in range(2))
        if upper is None:
            v = even + odd
            v = 0.125 * both(v[:, 0] + v[:, 1], 2, 2)
        else:
            g = lane // 32
            side = odd if upper else even
            first, second = (jnp.where(g == 1, side[:, d], even[:, d] + odd[:, d]) for d in range(2))
            v = jnp.where(g == 2, second if upper else first, first + second)
            v = 0.25 * jnp.where(g == 0, pick(v, 2, 2, upper), both(v, 2, 2))
        v = v.reshape(4, 4, 8, 128)
        out = v[:, 0]
        for u in range(1, 4):
            out = jnp.where(t == u, v[:, u], out)
        return out

    def z_gather(g, n):
        rows = pl.ds(pl.multiple_of(k * 32, 8), 32)
        return [remote(g.at[rows], g.at[rows], zg_send.at[n, u], zg_recv.at[n, u], gz=lax.rem(k + u, 8))
                for u in range(1, 8)]

    put(l3.up, 4 * k, third(l2.up, True))
    put(l3.low, 4 * k, third(l2.low, False))
    third_faces = z_gather(l3.up, 0) + z_gather(l3.low, 1)

    for copy in right_z:
        copy.wait_recv()
    yg1[j] = pz1[...]
    right_y = y_gather(pz1, yg1, 1)
    for copy in right_y:
        copy.start()
    for copy in third_faces:
        copy.start()
    for copy in third_faces:
        copy.wait_recv()
    make_coefs(l3, 32)
    for upper in (True, False):
        src, dst = (l3.up, l4.up) if upper else (l3.low, l4.low)

        def body(i, src=src, dst=dst, upper=upper):
            g = lane // 32
            v = l3.get(src, i)
            v = jnp.where(g == 2, pick(v, 1, 2, upper), both(v, 1, 2))
            v = jnp.where(g == 1, pick(v, 1, 1, upper), both(v, 1, 1))
            l4.put(dst, i, 0.25 * jnp.where(g == 0, pick(v, 4, 2, upper), both(v, 4, 2)))

        loop(l3.turns, body)
    make_coefs(l4, 32)
    for copy in right_y:
        copy.wait_recv()
    second_unpack(yg1, 0, l2.f)
    downward(l2)
    put(l3.f, 4 * k, third(l2.r))
    third_right = z_gather(l3.f, 2)
    for copy in third_right:
        copy.start()

    for copy in rx:
        copy.wait_recv()
    for g in range(8):
        v = slots(l0.r, 4 + 8 * g, 8)
        own = v[:, :8]
        own = jnp.where(slot // 2 == 1, roll(rxr[0].reshape(8, 8, 128), 2 - 2 * g, 2), own)
        own = jnp.where(slot // 2 == 6, roll(rxr[1].reshape(8, 8, 128), 12 - 2 * g, 2), own)
        put(l0.r, 4 + 8 * g, jnp.concatenate([own, v[:, 8:]], axis=1))
    edges0 = Wide(6, 8, l0.r, 0, 2)
    edges0.start()

    for copy in third_right:
        copy.wait_recv()

    downward(l3)

    def body(i):
        l4.put(l4.f, i, 0.125 * both(both(both(l3.get(l3.r, i), 1, 2), 1, 1), 4, 2))

    loop(l3.turns, body)
    solve_theta, solve_steps = SOLVE
    init_down(l4, solve_theta)
    w, w_next = l4.wa, l4.wb
    for n, (alpha, beta) in enumerate(solve_steps):
        step(l4, w, w_next, alpha, beta, last=n == len(solve_steps) - 1)
        w, w_next = w_next, w
    upward(l3, lambda i: l4.get(l4.x, i))

    for q in range(6):
        v = l3.x[pl.ds(pl.multiple_of(lax.rem(4 * k + q + 31, 32) * 8, 8), 8), :].reshape(1, 8, 128)
        for z in range(4):
            moved = v
            for u in range(4):
                if u != z:
                    moved = jnp.where(t == u, roll(v, u - z, 2), moved)
            first = (4 * q + z) * 16
            eb2[pl.ds(first, 8, stride=2), :] = moved.reshape(8, 128)
            eb2[pl.ds(first + 1, 8, stride=2), :] = moved.reshape(8, 128)

    def twice(ref, offset):
        def chunk(i):
            v = slots(ref, i * 4 + offset, 4)
            return jnp.broadcast_to(v[:, None], (4, 2, 16, 128)).reshape(8, 16, 128)

        return chunk

    upward(l2, twice(eb2, 0))

    for i, from_y in ((0, 0), (1, 1), (2, 2), (3, 3), (6, 14), (7, 15)):
        v = l2.x[pl.ds(lax.rem(2 * j + from_y, 16), 48, stride=16), :]
        eb1[pl.ds(2 * i, 48, stride=16), :] = v
        eb1[pl.ds(2 * i + 1, 48, stride=16), :] = v
    edges1.finish()
    upward(l1, twice(eb1, 6))
    edges = Wide(7, 4, l1.x, 0, 2)
    edges.start()
    edges0.finish()
    edges.finish()

    source = lax.broadcasted_iota(jnp.int32, (128, 128), 0)
    target = lax.broadcasted_iota(jnp.int32, (128, 128), 1)
    hit = (source // 32 == (target % 64) // 16) & (source % 32 == 4 * b - 2 + (target % 16) // 2)
    v = slots(l1.x, 0, 72)
    v = jnp.where(sub < 6, v[:, :8], v[:, 8:]).reshape(576, 128)
    v = jnp.dot(v, jnp.where(hit, 1.0, 0.0).astype(F32), precision=HIGHEST, preferred_element_type=F32)
    eb0[pl.ds(0, 576, stride=2), :] = v
    eb0[pl.ds(1, 576, stride=2), :] = v

    def top_chunk(i):
        v = jnp.where(lane16 < 64, slots(eb0, i * 4 + 2, 4), slots(eb0, i * 4 + 34, 4))
        return jnp.broadcast_to(v[:, None], (4, 2, 16, 128)).reshape(8, 16, 128)

    upward(l0, top_chunk)

    for y in range(0, 8, 2):
        first = l0.x[pl.ds(64 + y, 64, stride=16), :]
        second = l0.x[pl.ds(65 + y, 64, stride=16), :]
        low = jnp.where(half_lane, first, pltpu.roll(second, 64, 1))
        high = jnp.where(half_lane, pltpu.roll(first, 64, 1), second)
        turned = pltpu.roll(jnp.concatenate([low, high], axis=0), 124, 1).T
        for d in range(2):
            for v in range(4):
                start = d * 64 + v * 16
                out_ref[pl.ds(v * 64 + y + d, 8, stride=8), :] = turned[start:start + 8]

    for copy in (strips + [faces_first, right_first] + faces_second + right_second + rx + faces_z + right_z + faces_y
                 + right_y + third_faces + third_right):
        copy.wait_send()


def solution(mesh):
    def per_device(right_side, affinity):
        nx = affinity.shape[1] * mesh.shape["gx"]
        ny = affinity.shape[2] * mesh.shape["gy"]
        nz = affinity.shape[3] * mesh.shape["gz"]
        scratch = []
        for z, rows, *_ in LEVELS:
            scratch += level_shapes(z, rows)
        scratch += [pltpu.VMEM(shape, F32) for shape in (
            (4, 16, 8, 128), (4, 16, 8, 128),
            (8, 2, 4, 64, 128), (8, 2, 4, 64, 128), (8, 2, 32, 128), (8, 2, 3, 32, 128),
            (256, 128), (512, 128), (8, 32, 128), (8, 64, 128), (2, 64, 128), (2, 64, 128),
            (48, 128), (96, 128), (8, 48, 128), (8, 96, 128), (384, 128), (768, 128), (1152, 128))]
        dma = pltpu.SemaphoreType.DMA
        scratch += [dma(shape) for shape in (
            (2,), (4,), (4,), (8, 8), (8, 8), (2, 4), (2, 4), (2,), (2,), (3, 2), (3, 2), (2, 8), (2, 8), (3, 8), (3, 8))]
        out = pl.pallas_call(
            functools.partial(kernel, nx, ny, nz),
            out_shape=jax.ShapeDtypeStruct((256, 128), F32),
            in_specs=[pl.BlockSpec(memory_space=pl.ANY)] * 2,
            out_specs=pl.BlockSpec(memory_space=pltpu.VMEM),
            scratch_shapes=scratch,
            compiler_params=pltpu.CompilerParams(
                collective_id=0, has_side_effects=True, vmem_limit_bytes=60 * 1024 * 1024),
        )(right_side, affinity)
        return out.reshape(right_side.shape)

    spec = P(None, "gx", "gy", "gz")
    return jax.shard_map(per_device, mesh=mesh, in_specs=(spec, spec), out_specs=spec, check_vma=False)
```

time: 1040 us -> 148 us (0.14); the launches traced: 1020 us -> 148 us
  blocking collectives: 348 us -> 0 us
  starting transfers between devices: 320 us -> 0 us
  waiting for transfers between devices: 293 us -> 0 us
  Pallas kernels: 0 us -> 146 us
  local copies, waits for them, and re-layouts: 35.8 us -> 1.57 us
  other arithmetic: 25.3 us -> 0 us
    all_gather x4 -> x0, blocking collectives: 348 us -> none  [the longest x1 118 us: per_device(): lax.all_gather(faces_fourth[None], ('gy', 'gz'), axis=0, tiled=True)]
    ppermute x102 -> x0, starting transfers between devices: 320 us -> none  [the longest x51 239 us: extended(): lax.ppermute(lax.slice_in_dim(block, block.shape[dim] - width, None, axis...]
    ppermute x102 -> x0, waiting for transfers between devices: 293 us -> none  [the longest x51 279 us: extended(): lax.ppermute(lax.slice_in_dim(block, 0, width, axis=dim), axis, backward)]
    pallas_call x0 -> x1, Pallas kernels: none -> 146 us  [per_device(): pl.pallas_call(functools.partial(kernel, nx, ny, nz), out_shape=jax.Shape...]
    reduce_sum x33 -> x0, other arithmetic: 14.8 us -> none  [the longest x5 10.4 us: restrict(): return 0.125 * jnp.sum(grouped, axis=(depth + 1, depth + 3, depth + 5))]
  transfers between devices with their start and end apart: 102 -> 0, of which waited for: 56 -> 0; matrix products, arithmetic and copies ran while one was open for 1% -> 0% of each run, Pallas kernels for 0% -> 0%
where the time goes in v1:
time: 148 us
  Pallas kernels  146 us (99%)
  local copies, waits for them, and re-layouts  1.57 us (1%)
    pallas_call x1, Pallas kernels, per_device(): pl.pallas_call(functools.partial(kernel, nx, ny, nz), out_shape=jax.Shape...  146 us

profile of v1, /device:TPU:1, one launch (start us, length us, event | category | flops | bytes accessed | tf_op | source)
XLA Modules:
  0.0 147.7 jit_solution(15634991906642549665)
XLA Ops:
  0.0 146.1 %shard_map.28 = f32[256,128]{1,0:T(8,128)} custom-call(f32[4,8,8,128]{3,2,1,0:T(8,128)} %f_hbm.1, f32[3,8,8,128]{3,2,1,0:T(8,128)} %a_hbm.1), custom_call_target="tpu_custom_call" | custom-call | tf_op jit(solution)/shard_map/pallas_call | solution.py:734
  146.1 1.6 %copy.4 = f32[4,8,8,128]{3,2,1,0:T(8,128)} copy(f32[4,8,8,128]{3,2,1,0:T(8,128)} %bitcast.1) | data formatting | bytes 262144

commit v2 on v1

--- a/solution.py
+++ b/solution.py
@@ -84,8 +84,21 @@
     def __init__(self, z, rows, sy, sx, mode, refs):
         self.z, self.rows, self.sy, self.sx, self.mode = z, rows, sy, sx, mode
         self.ch = 128 // rows
-        self.turns = z // self.ch
-        (self.coef, self.scale, self.f, self.r, self.d, self.x, self.wa, self.wb, self.up, self.low) = refs
+        self.parts = z // self.ch if rows == 8 else 3
+        (self.coef, self.scale, self.f, self.r, self.d, self.x, self.wa, self.wb, self.up, self.low,
+         self.r_next, self.d_next, self.x_next) = refs
+
+    def loop(self, body):
+        def turn(i, carry):
+            for part in range(self.parts):
+                body(i * self.parts + part)
+            return carry
+
+        turns = self.z // (self.ch * self.parts)
+        if turns == 1:
+            turn(0, 0)
+        else:
+            lax.fori_loop(0, turns, turn, 0)
 
     def get(self, ref, i, offset=0):
         return slots(ref, i * self.ch + offset, self.ch, self.rows)
@@ -101,7 +114,7 @@
     n = z * rows
     pad = (z + 2) * rows
     return [pltpu.VMEM((6 * n, 128), F32)] + [pltpu.VMEM((n, 128), F32)] * 5 + [pltpu.VMEM((pad, 128), F32)] * 2 + [
-        pltpu.VMEM((n, 128), F32)] * 2
+        pltpu.VMEM((n, 128), F32)] * 5
 
 
 def neighbours(lv, w_ref, i):
@@ -136,17 +149,18 @@
         lv.put(lv.x, i, d)
         lv.put(lv.wa, i, lv.get(lv.scale, i) * d, 1)
 
-    loop(lv.turns, body)
+    lv.loop(body)
 
 
 def init_up(lv, coarse_at):
     def body(i):
         d = coarse_at(i)
         lv.put(lv.d, i, d)
-        lv.put(lv.x, i, lv.get(lv.x, i) + d)
+        lv.put(lv.x_next, i, lv.get(lv.x, i) + d)
         lv.put(lv.wa, i, lv.get(lv.scale, i) * d, 1)
 
-    loop(lv.turns, body)
+    lv.loop(body)
+    lv.x, lv.x_next = lv.x_next, lv.x
 
 
 def step(lv, w_ref, w_next, alpha=None, beta=None, last=False):
@@ -154,16 +168,21 @@
         d = lv.get(lv.d, i)
         r = lv.get(lv.r, i) - ((1.0 + SHIFT) * d - apply_at(lv, w_ref, i))
         if not last:
-            lv.put(lv.r, i, r)
+            lv.put(lv.r_next, i, r)
         if beta is None:
             return
         d = beta * r if alpha is None else alpha * d + beta * r
-        lv.put(lv.x, i, lv.get(lv.x, i) + d)
+        lv.put(lv.x_next, i, lv.get(lv.x, i) + d)
         if not last:
-            lv.put(lv.d, i, d)
+            lv.put(lv.d_next, i, d)
             lv.put(w_next, i, lv.get(lv.scale, i) * d, 1)
 
-    loop(lv.turns, body)
+    lv.loop(body)
+    if not last:
+        lv.r, lv.r_next = lv.r_next, lv.r
+    if beta is not None:
+        lv.x, lv.x_next = lv.x_next, lv.x
+        lv.d, lv.d_next = lv.d_next, lv.d
 
 
 def make_coefs(lv, group):
@@ -187,7 +206,7 @@
         for k in range(6):
             put(lv.coef, k * lv.z + i * lv.ch, scale * faces[k])
 
-    loop(lv.turns, body)
+    lv.loop(body)
 
 
 def own_pairs(ref, i):
@@ -212,7 +231,7 @@
         del refs[:count]
         return got
 
-    levels = [Level(*shape, take(10)) for shape in LEVELS]
+    levels = [Level(*shape, take(13)) for shape in LEVELS]
     (fext, aext, ys, yr, zs, zr, tb, tmp, xg1, xgf, rxs, rxr, pz1, pzf, yg1, ygf, eb2, eb1, eb0) = take(19)
     (local_sem, strip_send, strip_recv, ex_send, ex_recv, xg_send, xg_recv, rx_send, rx_recv,
      pz_send, pz_recv, yg_send, yg_recv, zg_send, zg_recv) = take(15)
@@ -243,6 +262,9 @@
     fext[:, 0] = jnp.zeros((4, 8, 128), F32)
     fext[:, 15] = jnp.zeros((4, 8, 128), F32)
     aext[3] = jnp.zeros((16, 8, 128), F32)
+    for n in (1, 2):
+        aext[n, 0] = jnp.zeros((8, 128), F32)
+        aext[n, 15] = jnp.zeros((8, 128), F32)
     for ref in (l0.f, l0.wa, l1.f, l1.up, l1.low, eb1):
         ref[...] = jnp.zeros_like(ref)
     for lv in levels:
@@ -253,16 +275,22 @@
 
     b_up, b_down = lax.rem(b + 1, 8), lax.rem(b + 7, 8)
     strips = [
-        remote(a_hbm.at[:, pl.ds(4, 4)], aext.at[pl.ds(0, 3), pl.ds(0, 4)],
+        remote(a_hbm.at[:, pl.ds(5, 3)], aext.at[pl.ds(0, 3), pl.ds(1, 3)],
                strip_send.at[0], strip_recv.at[0], gx=b_up),
-        remote(a_hbm.at[:, pl.ds(0, 4)], aext.at[pl.ds(0, 3), pl.ds(12, 4)],
+        remote(a_hbm.at[:, pl.ds(0, 3)], aext.at[pl.ds(0, 3), pl.ds(12, 3)],
                strip_send.at[1], strip_recv.at[1], gx=b_down),
+        remote(a_hbm.at[0, 4], aext.at[0, 0], strip_send.at[4], strip_recv.at[4], gx=b_up),
+        remote(a_hbm.at[0, 3], aext.at[0, 15], strip_send.at[5], strip_recv.at[5], gx=b_down),
         remote(f_hbm.at[:, pl.ds(5, 3)], fext.at[:, pl.ds(1, 3)],
                strip_send.at[2], strip_recv.at[2], gx=b_up),
         remote(f_hbm.at[:, pl.ds(0, 3)], fext.at[:, pl.ds(12, 3)],
                strip_send.at[3], strip_recv.at[3], gx=b_down),
     ]
-    for copy in strips:
+    for copy in strips[:4]:
+        copy.start()
+    for copy in strips[:4]:
+        copy.wait_send()
+    for copy in strips[4:]:
         copy.start()
 
     class Wide:
@@ -410,8 +438,8 @@
             dst[pl.ds(64 + i, 64, stride=16), :] = tmp[pl.ds(2 * i, 64, stride=8), :]
 
     own_a.wait()
-    strips[0].wait_recv()
-    strips[1].wait_recv()
+    for copy in strips[:4]:
+        copy.wait_recv()
     to_tiles(aext_rows, l0.wa, 1)
     edges = Wide(0, 8, l0.wa, 1, 4)
     edges.start()
@@ -431,7 +459,7 @@
         l0.put(l0.up, i, jnp.where(where == end, 0.0, 0.5 * (a + side_up)))
         l0.put(l0.low, i, jnp.where(where == 0, 0.0, 0.5 * (a + side_low)))
 
-    loop(l0.turns, face_body)
+    l0.loop(face_body)
 
     for upper, ref in ((True, l0.up), (False, l0.low)):
         def body(i, ref=ref, upper=upper):
@@ -444,14 +472,11 @@
     make_coefs(l0, 16)
 
     own_f.wait()
-    strips[2].wait_recv()
-    strips[3].wait_recv()
+    for copy in strips[4:]:
+        copy.wait_recv()
     to_tiles(fext_rows, l0.f, 0)
     edges = Wide(1, 8, l0.f, 0, 3)
     edges.start()
-    faces_first.wait_recv()
-    for copy in faces_second:
-        copy.start()
     edges.finish()
 
     over_theta, ((a1, b1), (a2, b2)) = SMOOTH
@@ -478,6 +503,9 @@
     x_pack(0.125, xg1, 0)
     right_first, right_second = x_gather(xg1, 0)
     right_first.start()
+    faces_first.wait_recv()
+    for copy in faces_second:
+        copy.start()
 
     slot = lane % 16
     for side, first in ((0, 10), (1, 4)):
@@ -540,16 +568,11 @@
     right_first.wait_recv()
     for copy in right_second:
         copy.start()
-    for copy in faces_y:
-        copy.wait_recv()
-    second_unpack(ygf, 0, l2.up)
-    second_unpack(ygf, 48, l2.low)
     for copy in right_second:
         copy.wait_recv()
     x_unpack(xg1, 0, l1.f)
     edges = Wide(4, 4, l1.f, 0, 3)
     edges.start()
-    make_coefs(l2, 32)
     edges.finish()
     downward(l1)
 
@@ -564,6 +587,11 @@
         copy.start()
     edges1 = Wide(5, 4, l1.r, 0, 2)
     edges1.start()
+
+    for copy in faces_y:
+        copy.wait_recv()
+    second_unpack(ygf, 0, l2.up)
+    second_unpack(ygf, 48, l2.low)
 
     t = lane % 4
 
@@ -601,6 +629,7 @@
         copy.start()
     for copy in third_faces:
         copy.start()
+    make_coefs(l2, 32)
     for copy in third_faces:
         copy.wait_recv()
     make_coefs(l3, 32)
@@ -614,7 +643,7 @@
             v = jnp.where(g == 1, pick(v, 1, 1, upper), both(v, 1, 1))
             l4.put(dst, i, 0.25 * jnp.where(g == 0, pick(v, 4, 2, upper), both(v, 4, 2)))
 
-        loop(l3.turns, body)
+        l3.loop(body)
     make_coefs(l4, 32)
     for copy in right_y:
         copy.wait_recv()
@@ -644,7 +673,7 @@
     def body(i):
         l4.put(l4.f, i, 0.125 * both(both(both(l3.get(l3.r, i), 1, 2), 1, 1), 4, 2))
 
-    loop(l3.turns, body)
+    l3.loop(body)
     solve_theta, solve_steps = SOLVE
     init_down(l4, solve_theta)
     w, w_next = l4.wa, l4.wb
@@ -710,7 +739,7 @@
                 start = d * 64 + v * 16
                 out_ref[pl.ds(v * 64 + y + d, 8, stride=8), :] = turned[start:start + 8]
 
-    for copy in (strips + [faces_first, right_first] + faces_second + right_second + rx + faces_z + right_z + faces_y
+    for copy in (strips[4:] + [faces_first, right_first] + faces_second + right_second + rx + faces_z + right_z + faces_y
                  + right_y + third_faces + third_right):
         copy.wait_send()
 
@@ -730,7 +759,7 @@
             (48, 128), (96, 128), (8, 48, 128), (8, 96, 128), (384, 128), (768, 128), (1152, 128))]
         dma = pltpu.SemaphoreType.DMA
         scratch += [dma(shape) for shape in (
-            (2,), (4,), (4,), (8, 8), (8, 8), (2, 4), (2, 4), (2,), (2,), (3, 2), (3, 2), (2, 8), (2, 8), (3, 8), (3, 8))]
+            (2,), (6,), (6,), (8, 8), (8, 8), (2, 4), (2, 4), (2,), (2,), (3, 2), (3, 2), (2, 8), (2, 8), (3, 8), (3, 8))]
         out = pl.pallas_call(
             functools.partial(kernel, nx, ny, nz),
             out_shape=jax.ShapeDtypeStruct((256, 128), F32),

time: 148 us -> 132 us (0.89)
  Pallas kernels: 146 us -> 130 us
    pallas_call x1, Pallas kernels: 146 us -> 130 us  [per_device(): pl.pallas_call(functools.partial(kernel, nx, ny, nz), out_shape=jax.Shape...]
where the time goes in v2:
time: 132 us
  Pallas kernels  130 us (98%)
  local copies, waits for them, and re-layouts  1.57 us (1%)
    pallas_call x1, Pallas kernels, per_device(): pl.pallas_call(functools.partial(kernel, nx, ny, nz), out_shape=jax.Shape...  130 us

profile of v2, /device:TPU:1, one launch (start us, length us, event | category | flops | bytes accessed | tf_op | source)
XLA Modules:
  0.0 131.5 jit_solution(10130450189552179693)
XLA Ops:
  0.0 129.9 %shard_map.28 = f32[256,128]{1,0:T(8,128)} custom-call(f32[4,8,8,128]{3,2,1,0:T(8,128)} %f_hbm.1, f32[3,8,8,128]{3,2,1,0:T(8,128)} %a_hbm.1), custom_call_target="tpu_custom_call" | custom-call | tf_op jit(solution)/shard_map/pallas_call | solution.py:763
  129.9 1.6 %copy.4 = f32[4,8,8,128]{3,2,1,0:T(8,128)} copy(f32[4,8,8,128]{3,2,1,0:T(8,128)} %bitcast.1) | data formatting | bytes 262144

commit v3 on v2

--- a/solution.py
+++ b/solution.py
@@ -85,8 +85,8 @@
         self.z, self.rows, self.sy, self.sx, self.mode = z, rows, sy, sx, mode
         self.ch = 128 // rows
         self.parts = z // self.ch if rows == 8 else 3
-        (self.coef, self.scale, self.f, self.r, self.d, self.x, self.wa, self.wb, self.up, self.low,
-         self.r_next, self.d_next, self.x_next) = refs
+        (self.coef, self.scale, self.root, self.f, self.r, self.x, self.wa, self.wb, self.up, self.low,
+         self.r_next, self.x_next) = refs
 
     def loop(self, body):
         def turn(i, carry):
@@ -114,7 +114,7 @@
     n = z * rows
     pad = (z + 2) * rows
     return [pltpu.VMEM((6 * n, 128), F32)] + [pltpu.VMEM((n, 128), F32)] * 5 + [pltpu.VMEM((pad, 128), F32)] * 2 + [
-        pltpu.VMEM((n, 128), F32)] * 5
+        pltpu.VMEM((n, 128), F32)] * 4
 
 
 def neighbours(lv, w_ref, i):
@@ -131,58 +131,48 @@
     return w, xd, xu, yd, yu, zd, zu
 
 
-def apply_at(lv, w_ref, i):
-    _, *near = neighbours(lv, w_ref, i)
-    total = None
-    for k, value in enumerate(near):
-        term = slots(lv.coef, k * lv.z + i * lv.ch, lv.ch, lv.rows) * value
-        total = term if total is None else total + term
-    return total
-
-
 def init_down(lv, over_theta):
     def body(i):
-        f = lv.get(lv.f, i)
-        d = f * over_theta
-        lv.put(lv.r, i, f)
-        lv.put(lv.d, i, d)
-        lv.put(lv.x, i, d)
-        lv.put(lv.wa, i, lv.get(lv.scale, i) * d, 1)
+        r = lv.get(lv.scale, i) * lv.get(lv.f, i)
+        lv.put(lv.r, i, r)
+        lv.put(lv.wa, i, r * over_theta, 1)
 
     lv.loop(body)
 
 
 def init_up(lv, coarse_at):
     def body(i):
-        d = coarse_at(i)
-        lv.put(lv.d, i, d)
-        lv.put(lv.x_next, i, lv.get(lv.x, i) + d)
-        lv.put(lv.wa, i, lv.get(lv.scale, i) * d, 1)
+        lv.put(lv.wa, i, lv.get(lv.scale, i) * coarse_at(i), 1)
 
     lv.loop(body)
-    lv.x, lv.x_next = lv.x_next, lv.x
-
-
-def step(lv, w_ref, w_next, alpha=None, beta=None, last=False):
+
+
+def step(lv, w_ref, w_next, alpha=None, beta=None, add="", last=False):
     def body(i):
-        d = lv.get(lv.d, i)
-        r = lv.get(lv.r, i) - ((1.0 + SHIFT) * d - apply_at(lv, w_ref, i))
+        w, *near = neighbours(lv, w_ref, i)
+        total = None
+        for k, value in enumerate(near):
+            term = slots(lv.coef, k * lv.z + i * lv.ch, lv.ch, lv.rows) * value
+            total = term if total is None else total + term
+        r = lv.get(lv.r, i) - ((1.0 + SHIFT) * w - total)
         if not last:
             lv.put(lv.r_next, i, r)
         if beta is None:
             return
-        d = beta * r if alpha is None else alpha * d + beta * r
-        lv.put(lv.x_next, i, lv.get(lv.x, i) + d)
+        new = beta * r if alpha is None else alpha * w + beta * r
+        if add:
+            x = new + w if "w" in add else new
+            if "x" in add:
+                x = x + lv.get(lv.x, i)
+            lv.put(lv.x_next, i, x * lv.get(lv.root, i) if last else x)
         if not last:
-            lv.put(lv.d_next, i, d)
-            lv.put(w_next, i, lv.get(lv.scale, i) * d, 1)
+            lv.put(w_next, i, new, 1)
 
     lv.loop(body)
     if not last:
         lv.r, lv.r_next = lv.r_next, lv.r
-    if beta is not None:
+    if add:
         lv.x, lv.x_next = lv.x_next, lv.x
-        lv.d, lv.d_next = lv.d_next, lv.d
 
 
 def make_coefs(lv, group):
@@ -203,8 +193,10 @@
         total = faces[0] + faces[1] + faces[2] + faces[3] + faces[4] + faces[5]
         scale = jnp.where(total > 0.0, lax.rsqrt(total), 0.0)
         lv.put(lv.scale, i, scale)
+        lv.put(lv.root, i, scale * total)
+        square = scale * scale
         for k in range(6):
-            put(lv.coef, k * lv.z + i * lv.ch, scale * faces[k])
+            put(lv.coef, k * lv.z + i * lv.ch, square * faces[k])
 
     lv.loop(body)
 
@@ -231,7 +223,7 @@
         del refs[:count]
         return got
 
-    levels = [Level(*shape, take(13)) for shape in LEVELS]
+    levels = [Level(*shape, take(12)) for shape in LEVELS]
     (fext, aext, ys, yr, zs, zr, tb, tmp, xg1, xgf, rxs, rxr, pz1, pzf, yg1, ygf, eb2, eb1, eb0) = take(19)
     (local_sem, strip_send, strip_recv, ex_send, ex_recv, xg_send, xg_recv, rx_send, rx_recv,
      pz_send, pz_recv, yg_send, yg_recv, zg_send, zg_recv) = take(15)
@@ -461,6 +453,12 @@
 
     l0.loop(face_body)
 
+    own_f.wait()
+    for copy in strips[4:]:
+        copy.wait_recv()
+    to_tiles(fext_rows, l0.f, 0)
+    edges = Wide(1, 8, l0.f, 0, 3)
+    edges.start()
     for upper, ref in ((True, l0.up), (False, l0.low)):
         def body(i, ref=ref, upper=upper):
             put(tb, i * 16, coarse_faces(*own_pairs(ref, i), 16, upper, 1, None))
@@ -471,33 +469,30 @@
     faces_first.start()
     make_coefs(l0, 16)
 
-    own_f.wait()
-    for copy in strips[4:]:
-        copy.wait_recv()
-    to_tiles(fext_rows, l0.f, 0)
-    edges = Wide(1, 8, l0.f, 0, 3)
-    edges.start()
     edges.finish()
 
     over_theta, ((a1, b1), (a2, b2)) = SMOOTH
 
     def downward(lv):
         init_down(lv, over_theta)
-        step(lv, lv.wa, lv.wb, a1, b1)
-        step(lv, lv.wb, lv.wa, a2, b2)
+        step(lv, lv.wa, lv.wb, a1, b1, add="w")
+        step(lv, lv.wb, lv.wa, a2, b2, add="x")
         step(lv, lv.wa, None)
 
     def upward(lv, coarse_at):
         init_up(lv, coarse_at)
-        step(lv, lv.wa, lv.wb, None, over_theta)
+        step(lv, lv.wa, lv.wb, None, over_theta, add="xw")
         step(lv, lv.wb, lv.wa, a1, b1)
-        step(lv, lv.wa, None, a2, b2, last=True)
+        step(lv, lv.wa, None, a2, b2, add="xw", last=True)
+
+    def own_sums(lv, i):
+        pairs, roots = own_pairs(lv.r, i), own_pairs(lv.root, i)
+        return pairs[0] * roots[0] + pairs[1] * roots[1]
 
     downward(l0)
 
     def body(i):
-        first, second = own_pairs(l0.r, i)
-        put(tb, i * 16, both(first + second, 1, 1))
+        put(tb, i * 16, both(own_sums(l0, i), 1, 1))
 
     loop(2, body)
     x_pack(0.125, xg1, 0)
@@ -557,6 +552,9 @@
         copy.start()
     edges_up.finish()
     edges_low.finish()
+    right_first.wait_recv()
+    for copy in right_second:
+        copy.start()
     make_coefs(l1, 32)
     for copy in faces_z:
         copy.wait_recv()
@@ -565,9 +563,6 @@
     for copy in faces_y:
         copy.start()
 
-    right_first.wait_recv()
-    for copy in right_second:
-        copy.start()
     for copy in right_second:
         copy.wait_recv()
     x_unpack(xg1, 0, l1.f)
@@ -577,8 +572,7 @@
     downward(l1)
 
     def body(i):
-        first, second = own_pairs(l1.r, i)
-        put(tb, i * 16, 0.125 * both(both(first + second, 1, 1), 1, 2))
+        put(tb, i * 16, 0.125 * both(both(own_sums(l1, i), 1, 1), 1, 2))
 
     loop(2, body)
     second_pack(pz1, 0)
@@ -598,7 +592,8 @@
     def third(ref, upper=None):
         even, odd = (ref[pl.ds(128 + d, 256, stride=2), :].reshape(16, 2, 8, 128) for d in range(2))
         if upper is None:
-            v = even + odd
+            roots = [l2.root[pl.ds(128 + d, 256, stride=2), :].reshape(16, 2, 8, 128) for d in range(2)]
+            v = even * roots[0] + odd * roots[1]
             v = 0.125 * both(v[:, 0] + v[:, 1], 2, 2)
         else:
             g = lane // 32
@@ -671,14 +666,14 @@
     downward(l3)
 
     def body(i):
-        l4.put(l4.f, i, 0.125 * both(both(both(l3.get(l3.r, i), 1, 2), 1, 1), 4, 2))
+        l4.put(l4.f, i, 0.125 * both(both(both(l3.get(l3.r, i) * l3.get(l3.root, i), 1, 2), 1, 1), 4, 2))
 
     l3.loop(body)
     solve_theta, solve_steps = SOLVE
     init_down(l4, solve_theta)
     w, w_next = l4.wa, l4.wb
     for n, (alpha, beta) in enumerate(solve_steps):
-        step(l4, w, w_next, alpha, beta, last=n == len(solve_steps) - 1)
+        step(l4, w, w_next, alpha, beta, add="x" if n else "w", last=n == len(solve_steps) - 1)
         w, w_next = w_next, w
     upward(l3, lambda i: l4.get(l4.x, i))
 

time: 132 us -> 129 us (0.977)
  Pallas kernels: 130 us -> 127 us
    pallas_call x1, Pallas kernels: 130 us -> 127 us  [per_device(): pl.pallas_call(functools.partial(kernel, nx, ny, nz), out_shape=jax.Shape...]
where the time goes in v3:
time: 129 us
  Pallas kernels  127 us (98%)
  local copies, waits for them, and re-layouts  1.57 us (1%)
    pallas_call x1, Pallas kernels, per_device(): pl.pallas_call(functools.partial(kernel, nx, ny, nz), out_shape=jax.Shape...  127 us

profile of v3, /device:TPU:1, one launch (start us, length us, event | category | flops | bytes accessed | tf_op | source)
XLA Modules:
  0.0 128.7 jit_solution(17414229372922793001)
XLA Ops:
  0.0 127.1 %shard_map.28 = f32[256,128]{1,0:T(8,128)} custom-call(f32[4,8,8,128]{3,2,1,0:T(8,128)} %f_hbm.1, f32[3,8,8,128]{3,2,1,0:T(8,128)} %a_hbm.1), custom_call_target="tpu_custom_call" | custom-call | tf_op jit(solution)/shard_map/pallas_call | solution.py:758
  127.1 1.6 %copy.4 = f32[4,8,8,128]{3,2,1,0:T(8,128)} copy(f32[4,8,8,128]{3,2,1,0:T(8,128)} %bitcast.1) | data formatting | bytes 262144

commit v4 on v3

--- a/solution.py
+++ b/solution.py
@@ -224,9 +224,9 @@
         return got
 
     levels = [Level(*shape, take(12)) for shape in LEVELS]
-    (fext, aext, ys, yr, zs, zr, tb, tmp, xg1, xgf, rxs, rxr, pz1, pzf, yg1, ygf, eb2, eb1, eb0) = take(19)
+    (fext, aext, ys, yr, zs, zr, tb, tmp, xg1, xgf, rxs, rxr, q1, qf, yg1, ygf, zh1, zhf, eb2, eb1, eb0) = take(21)
     (local_sem, strip_send, strip_recv, ex_send, ex_recv, xg_send, xg_recv, rx_send, rx_recv,
-     pz_send, pz_recv, yg_send, yg_recv, zg_send, zg_recv) = take(15)
+     h_send, h_recv, yg_send, yg_recv, yc_send, yc_recv, zg_send, zg_recv) = take(17)
     l0, l1, l2, l3, l4 = levels
 
     b, j, k = lax.axis_index("gx"), lax.axis_index("gy"), lax.axis_index("gz")
@@ -511,8 +511,6 @@
         rxs[side] = packed.reshape(64, 128)
     rx = [remote(rxs.at[0], rxr.at[0], rx_send.at[0], rx_recv.at[0], gx=b_up),
           remote(rxs.at[1], rxr.at[1], rx_send.at[1], rx_recv.at[1], gx=b_down)]
-    for copy in rx:
-        copy.start()
 
     for copy in faces_second:
         copy.wait_recv()
@@ -522,22 +520,25 @@
     edges_up.start()
     edges_low.start()
 
-    def second_pack(pz, first):
-        v = jnp.where(lane2 % 2 == 0, tb[pl.ds(0, 32, stride=8), :], tb[pl.ds(2, 32, stride=8), :])
-        pz[pl.ds(first + 8, 32), :] = v
-
-    def second_edges(pz, first, n):
-        up, down = pl.ds(first + 32, 8), pl.ds(first + 8, 8)
-        return [remote(pz.at[up], pz.at[pl.ds(first, 8)], pz_send.at[n, 0], pz_recv.at[n, 0], gz=lax.rem(k + 1, 8)),
-                remote(pz.at[down], pz.at[pl.ds(first + 40, 8)], pz_send.at[n, 1], pz_recv.at[n, 1],
-                       gz=lax.rem(k + 7, 8))]
-
-    def y_gather(pz, yg, n):
-        return [remote(pz, yg.at[j], yg_send.at[n, t], yg_recv.at[n, t], gy=lax.rem(j + t, 8)) for t in range(1, 8)]
-
-    def second_unpack(yg, first, dst):
+    def second_pack(q, first):
+        start = pl.multiple_of((b // 2) * 64, 64)
+        q[pl.ds(first, 8), :] = jnp.where(lane2 % 2 == 0, tb[pl.ds(start, 8, stride=8), :],
+                                          tb[pl.ds(start + 2, 8, stride=8), :])
+
+    def second_gather(q, yg, zh, n):
+        c = b // 2
+        along = [remote(q, yg.at[c, j], yg_send.at[n, t], yg_recv.at[n, t], gy=lax.rem(j + t, 8)) for t in range(1, 8)]
+        quarters = [remote(yg.at[c], yg.at[c], yc_send.at[n, t], yc_recv.at[n, t], gx=lax.rem(b + 2 * t, 8))
+                    for t in range(1, 4)]
+        halo = [remote(yg.at[3], zh.at[0], h_send.at[n, 0], h_recv.at[n, 0], gz=lax.rem(k + 1, 8)),
+                remote(yg.at[0], zh.at[1], h_send.at[n, 1], h_recv.at[n, 1], gz=lax.rem(k + 7, 8))]
+        return along, quarters, halo
+
+    def second_unpack(yg, zh, first, dst):
+        rows = pl.ds(first, 8)
         for n in range(8):
-            v = yg[n, pl.ds(first, 48), :]
+            parts = [zh[0, n, rows, :]] + [yg[c, n, rows, :] for c in range(4)] + [zh[1, n, rows, :]]
+            v = jnp.concatenate(parts, axis=0)
             dst[pl.ds(2 * n, 48, stride=16), :] = jnp.where(lane2 % 2 == 0, v, roll(v, 1, 1))
             dst[pl.ds(2 * n + 1, 48, stride=16), :] = jnp.where(lane2 % 2 == 1, v, roll(v, -1, 1))
 
@@ -546,22 +547,17 @@
             put(tb, i * 16, 0.25 * coarse_faces(*own_pairs(ref, i), 32, upper, 1, 1))
 
         loop(2, body)
-        second_pack(pzf, 0 if upper else 48)
-    faces_z = second_edges(pzf, 0, 0) + second_edges(pzf, 48, 1)
-    for copy in faces_z:
-        copy.start()
+        second_pack(qf, 0 if upper else 8)
+    ygf[b // 2, j] = qf[...]
+    faces_y, faces_c, faces_h = second_gather(qf, ygf, zhf, 0)
     edges_up.finish()
     edges_low.finish()
     right_first.wait_recv()
     for copy in right_second:
         copy.start()
+    for copy in faces_y:
+        copy.start()
     make_coefs(l1, 32)
-    for copy in faces_z:
-        copy.wait_recv()
-    ygf[j] = pzf[...]
-    faces_y = y_gather(pzf, ygf, 0)
-    for copy in faces_y:
-        copy.start()
 
     for copy in right_second:
         copy.wait_recv()
@@ -569,23 +565,29 @@
     edges = Wide(4, 4, l1.f, 0, 3)
     edges.start()
     edges.finish()
+    for copy in faces_y:
+        copy.wait_recv()
+    for copy in faces_c:
+        copy.start()
     downward(l1)
 
     def body(i):
         put(tb, i * 16, 0.125 * both(both(own_sums(l1, i), 1, 1), 1, 2))
 
     loop(2, body)
-    second_pack(pz1, 0)
-    right_z = second_edges(pz1, 0, 2)
-    for copy in right_z:
-        copy.start()
-    edges1 = Wide(5, 4, l1.r, 0, 2)
-    edges1.start()
-
-    for copy in faces_y:
-        copy.wait_recv()
-    second_unpack(ygf, 0, l2.up)
-    second_unpack(ygf, 48, l2.low)
+    second_pack(q1, 0)
+    yg1[b // 2, j] = q1[...]
+    right_y, right_c, right_h = second_gather(q1, yg1, zh1, 1)
+    for copy in right_y:
+        copy.start()
+    for copy in faces_c:
+        copy.wait_recv()
+    for copy in faces_h:
+        copy.start()
+    for copy in faces_h:
+        copy.wait_recv()
+    second_unpack(ygf, zhf, 0, l2.up)
+    second_unpack(ygf, zhf, 8, l2.low)
 
     t = lane % 4
 
@@ -616,15 +618,13 @@
     put(l3.low, 4 * k, third(l2.low, False))
     third_faces = z_gather(l3.up, 0) + z_gather(l3.low, 1)
 
-    for copy in right_z:
-        copy.wait_recv()
-    yg1[j] = pz1[...]
-    right_y = y_gather(pz1, yg1, 1)
+    for copy in third_faces:
+        copy.start()
+    make_coefs(l2, 32)
     for copy in right_y:
-        copy.start()
-    for copy in third_faces:
-        copy.start()
-    make_coefs(l2, 32)
+        copy.wait_recv()
+    for copy in right_c:
+        copy.start()
     for copy in third_faces:
         copy.wait_recv()
     make_coefs(l3, 32)
@@ -639,26 +639,23 @@
             l4.put(dst, i, 0.25 * jnp.where(g == 0, pick(v, 4, 2, upper), both(v, 4, 2)))
 
         l3.loop(body)
+    for copy in right_c:
+        copy.wait_recv()
+    for copy in right_h:
+        copy.start()
     make_coefs(l4, 32)
-    for copy in right_y:
-        copy.wait_recv()
-    second_unpack(yg1, 0, l2.f)
+    for copy in right_h:
+        copy.wait_recv()
+    second_unpack(yg1, zh1, 0, l2.f)
+    edges1 = Wide(5, 4, l1.r, 0, 2)
+    edges1.start()
+    for copy in rx:
+        copy.start()
     downward(l2)
     put(l3.f, 4 * k, third(l2.r))
     third_right = z_gather(l3.f, 2)
     for copy in third_right:
         copy.start()
-
-    for copy in rx:
-        copy.wait_recv()
-    for g in range(8):
-        v = slots(l0.r, 4 + 8 * g, 8)
-        own = v[:, :8]
-        own = jnp.where(slot // 2 == 1, roll(rxr[0].reshape(8, 8, 128), 2 - 2 * g, 2), own)
-        own = jnp.where(slot // 2 == 6, roll(rxr[1].reshape(8, 8, 128), 12 - 2 * g, 2), own)
-        put(l0.r, 4 + 8 * g, jnp.concatenate([own, v[:, 8:]], axis=1))
-    edges0 = Wide(6, 8, l0.r, 0, 2)
-    edges0.start()
 
     for copy in third_right:
         copy.wait_recv()
@@ -697,6 +694,17 @@
 
     upward(l2, twice(eb2, 0))
 
+    for copy in rx:
+        copy.wait_recv()
+    for g in range(8):
+        v = slots(l0.r, 4 + 8 * g, 8)
+        own = v[:, :8]
+        own = jnp.where(slot // 2 == 1, roll(rxr[0].reshape(8, 8, 128), 2 - 2 * g, 2), own)
+        own = jnp.where(slot // 2 == 6, roll(rxr[1].reshape(8, 8, 128), 12 - 2 * g, 2), own)
+        put(l0.r, 4 + 8 * g, jnp.concatenate([own, v[:, 8:]], axis=1))
+    edges0 = Wide(6, 8, l0.r, 0, 2)
+    edges0.start()
+
     for i, from_y in ((0, 0), (1, 1), (2, 2), (3, 3), (6, 14), (7, 15)):
         v = l2.x[pl.ds(lax.rem(2 * j + from_y, 16), 48, stride=16), :]
         eb1[pl.ds(2 * i, 48, stride=16), :] = v
@@ -734,8 +742,8 @@
                 start = d * 64 + v * 16
                 out_ref[pl.ds(v * 64 + y + d, 8, stride=8), :] = turned[start:start + 8]
 
-    for copy in (strips[4:] + [faces_first, right_first] + faces_second + right_second + rx + faces_z + right_z + faces_y
-                 + right_y + third_faces + third_right):
+    for copy in (strips[4:] + [faces_first, right_first] + faces_second + right_second + rx + faces_y + right_y + faces_c
+                 + right_c + faces_h + right_h + third_faces + third_right):
         copy.wait_send()
 
 
@@ -751,10 +759,10 @@
             (4, 16, 8, 128), (4, 16, 8, 128),
             (8, 2, 4, 64, 128), (8, 2, 4, 64, 128), (8, 2, 32, 128), (8, 2, 3, 32, 128),
             (256, 128), (512, 128), (8, 32, 128), (8, 64, 128), (2, 64, 128), (2, 64, 128),
-            (48, 128), (96, 128), (8, 48, 128), (8, 96, 128), (384, 128), (768, 128), (1152, 128))]
+            (8, 128), (16, 128), (4, 8, 8, 128), (4, 8, 16, 128), (2, 8, 8, 128), (2, 8, 16, 128), (384, 128), (768, 128), (1152, 128))]
         dma = pltpu.SemaphoreType.DMA
         scratch += [dma(shape) for shape in (
-            (2,), (6,), (6,), (8, 8), (8, 8), (2, 4), (2, 4), (2,), (2,), (3, 2), (3, 2), (2, 8), (2, 8), (3, 8), (3, 8))]
+            (2,), (6,), (6,), (8, 8), (8, 8), (2, 4), (2, 4), (2,), (2,), (2, 2), (2, 2), (2, 8), (2, 8), (2, 4), (2, 4), (3, 8), (3, 8))]
         out = pl.pallas_call(
             functools.partial(kernel, nx, ny, nz),
             out_shape=jax.ShapeDtypeStruct((256, 128), F32),

time: 129 us -> 120 us (0.930)
  Pallas kernels: 127 us -> 118 us
    pallas_call x1, Pallas kernels: 127 us -> 118 us  [per_device(): pl.pallas_call(functools.partial(kernel, nx, ny, nz), out_shape=jax.Shape...]
where the time goes in v4:
time: 120 us
  Pallas kernels  118 us (98%)
  local copies, waits for them, and re-layouts  1.57 us (1%)
    pallas_call x1, Pallas kernels, per_device(): pl.pallas_call(functools.partial(kernel, nx, ny, nz), out_shape=jax.Shape...  118 us

profile of v4, /device:TPU:1, one launch (start us, length us, event | category | flops | bytes accessed | tf_op | source)
XLA Modules:
  0.0 119.8 jit_solution(13838296894418594129)
XLA Ops:
  0.0 118.3 %shard_map.28 = f32[256,128]{1,0:T(8,128)} custom-call(f32[4,8,8,128]{3,2,1,0:T(8,128)} %f_hbm.1, f32[3,8,8,128]{3,2,1,0:T(8,128)} %a_hbm.1), custom_call_target="tpu_custom_call" | custom-call | tf_op jit(solution)/shard_map/pallas_call | solution.py:766
  118.3 1.6 %copy.4 = f32[4,8,8,128]{3,2,1,0:T(8,128)} copy(f32[4,8,8,128]{3,2,1,0:T(8,128)} %bitcast.1) | data formatting | bytes 262144

commit v5 on v4

--- a/solution.py
+++ b/solution.py
@@ -48,11 +48,9 @@
     return x + jnp.where(bit == 0, roll(x, -k, axis), roll(x, k, axis))
 
 
-def pick(x, k, axis, upper):
+def pick(x, k, axis):
     bit = (iota(axis, (1,) + x.shape[1:]) // k) % 2
-    if upper:
-        return jnp.where(bit == 1, x, roll(x, -k, axis))
-    return jnp.where(bit == 0, x, roll(x, k, axis))
+    return jnp.where(bit == 1, x, roll(x, -k, axis))
 
 
 def slots(ref, start, count, rows=16):
@@ -113,8 +111,8 @@
 def level_shapes(z, rows):
     n = z * rows
     pad = (z + 2) * rows
-    return [pltpu.VMEM((6 * n, 128), F32)] + [pltpu.VMEM((n, 128), F32)] * 5 + [pltpu.VMEM((pad, 128), F32)] * 2 + [
-        pltpu.VMEM((n, 128), F32)] * 4
+    return [pltpu.VMEM((6 * n, 128), F32)] + [pltpu.VMEM((n, 128), F32)] * 5 + [pltpu.VMEM((pad, 128), F32)] * 4 + [
+        pltpu.VMEM((n, 128), F32)] * 2
 
 
 def neighbours(lv, w_ref, i):
@@ -186,10 +184,15 @@
         return out
 
     def body(i):
-        low, up = lv.get(lv.low, i), lv.get(lv.up, i)
+        if group == 16:
+            up = lv.get(lv.up, i)
+            lows = [lv.get(lv.low, i)] * 3
+        else:
+            up, x_low, _, y_low, _, z_low, _ = neighbours(lv, lv.up, i)
+            lows = [jnp.where(iota(2, (1, lv.rows, 128)) % 32 < lv.sx, 0.0, x_low), y_low, z_low]
         faces = []
         for k in range(3):
-            faces += [spread(low, k), spread(up, k)]
+            faces += [spread(lows[k], k), spread(up, k)]
         total = faces[0] + faces[1] + faces[2] + faces[3] + faces[4] + faces[5]
         scale = jnp.where(total > 0.0, lax.rsqrt(total), 0.0)
         lv.put(lv.scale, i, scale)
@@ -201,18 +204,49 @@
     lv.loop(body)
 
 
-def own_pairs(ref, i):
-    v = slots(ref, 4 + 32 * i, 32)[:, :8].reshape(16, 2, 8, 128)
+def own_pairs(ref, i, base=0):
+    v = slots(ref, base + 4 + 32 * i, 32)[:, :8].reshape(16, 2, 8, 128)
     return v[:, 0], v[:, 1]
 
 
-def coarse_faces(first, second, group, upper, ky, kx):
+def coarse_faces(first, second, group, ky, kx):
     g = (iota(2) // group) % 4
-    v = jnp.where(g == 2, second if upper else first, first + second)
-    v = jnp.where(g == 1, pick(v, ky, 1, upper), both(v, ky, 1))
+    v = jnp.where(g == 2, second, first + second)
+    v = jnp.where(g == 1, pick(v, ky, 1), both(v, ky, 1))
     if kx is not None:
-        v = jnp.where(g == 0, pick(v, kx, 2, upper), both(v, kx, 2))
+        v = jnp.where(g == 0, pick(v, kx, 2), both(v, kx, 2))
     return v
+
+
+def own_step(lv, w_ref, alpha=None, beta=None):
+    def body(i):
+        first = 4 + 8 * i
+        here = slots(w_ref, first + 1, 8)
+        w = here[:, :8]
+        near = [roll(w, 1, 2), roll(w, -1, 2), roll(here, 1, 1)[:, :8], roll(here, -1, 1)[:, :8],
+                slots(w_ref, first, 8)[:, :8], slots(w_ref, first + 2, 8)[:, :8]]
+        total = None
+        for k, value in enumerate(near):
+            term = slots(lv.coef, k * lv.z + first, 8)[:, :8] * value
+            total = term if total is None else total + term
+        r = slots(lv.r, first, 8)[:, :8] - ((1.0 + SHIFT) * w - total)
+        if beta is not None:
+            x = slots(lv.x, first, 8)[:, :8] + w + (alpha * w + beta * r)
+            r = x * slots(lv.root, first, 8)[:, :8]
+        target = lv.r_next if beta is None else lv.x_next
+        for n in range(8):
+            target[pl.ds(pl.multiple_of((first + n) * 16, 16), 8), :] = r[n]
+
+    def turn(i, carry):
+        for part in range(4):
+            body(4 * i + part)
+        return carry
+
+    lax.fori_loop(0, 2, turn, 0)
+    if beta is None:
+        lv.r, lv.r_next = lv.r_next, lv.r
+    else:
+        lv.x, lv.x_next = lv.x_next, lv.x
 
 
 def kernel(nx, ny, nz, f_hbm, a_hbm, out_ref, *scratch):
@@ -248,6 +282,7 @@
     partners += [{"gy": lax.rem(j + t, 8)} for t in range(1, 8)]
     partners += [{"gz": lax.rem(k + t, 8)} for t in range(1, 8)]
     partners += [{"gy": lax.rem(j + t, 8), "gz": lax.rem(k + u, 8)} for t in (1, 7) for u in (1, 7)]
+    partners += [{"gx": lax.rem(b + t, 8), "gz": lax.rem(k + u, 8)} for t in (2, 4, 6) for u in (1, 7)]
     for to in partners:
         pl.semaphore_signal(barrier, inc=1, device_id=to, device_id_type=MESH)
 
@@ -257,10 +292,10 @@
     for n in (1, 2):
         aext[n, 0] = jnp.zeros((8, 128), F32)
         aext[n, 15] = jnp.zeros((8, 128), F32)
-    for ref in (l0.f, l0.wa, l1.f, l1.up, l1.low, eb1):
+    for ref in (l0.f, l0.wa, l1.f, l1.up, eb1):
         ref[...] = jnp.zeros_like(ref)
     for lv in levels:
-        for w in (lv.wa, lv.wb):
+        for w in (lv.wa, lv.wb, lv.up):
             w[pl.ds(0, lv.rows), :] = jnp.zeros((lv.rows, 128), F32)
             w[pl.ds((lv.z + 1) * lv.rows, lv.rows), :] = jnp.zeros((lv.rows, 128), F32)
     pl.semaphore_wait(barrier, len(partners))
@@ -390,14 +425,14 @@
                   for t in range(1, 4)]
         return first, second
 
-    def x_pack(weight, xg, first, upper=None):
+    def x_pack(weight, xg, faces=False):
         source = lax.broadcasted_iota(jnp.int32, (128, 256), 0)
         target = lax.broadcasted_iota(jnp.int32, (128, 256), 1)
         slot, inner = source % 16, (target % 128) % 32
         hit = (source // 64 == target // 128) & ((source % 64) // 16 == (target % 128) // 32) & (inner < 4)
         pair = (slot // 2 == inner + 2) & hit
-        if upper is not None:
-            pair = pair & (((source % 64) // 16 != 0) | (slot % 2 == (1 if upper else 0)))
+        if faces:
+            pair = pair & (((source % 64) // 16 != 0) | (slot % 2 == 1))
         matrix = jnp.where(pair, weight, 0.0).astype(F32)
         moved = jnp.dot(tb[...], matrix, precision=HIGHEST, preferred_element_type=F32)
         parts = [moved[:, :128].reshape(32, 8, 128), moved[:, 128:].reshape(32, 8, 128)]
@@ -406,15 +441,15 @@
             part = roll(parts[g // 4][(g % 4) * 8:(g % 4) * 8 + 8], 4 * g, 2)
             total = part if total is None else total + part
         packed = jnp.where(sub % 2 == 0, total[:4], total[4:])
-        xg[b, pl.ds(first * 8, 32), :] = packed.reshape(32, 128)
-
-    def x_unpack(xg, first, dst):
+        xg[b] = packed.reshape(32, 128)
+
+    def x_unpack(xg, dst, base):
         g = (lane // 4) % 8
         for q in range(4):
             for odd in range(2):
                 v = []
                 for n in range(8):
-                    tile = xg[n, pl.ds((first + q) * 8, 8), :].reshape(1, 8, 128)
+                    tile = xg[n, pl.ds(q * 8, 8), :].reshape(1, 8, 128)
                     v.append(jnp.where(sub % 2 == 1, tile, roll(tile, -1, 1)) if odd
                              else jnp.where(sub % 2 == 0, tile, roll(tile, 1, 1)))
                 for s in (1, 2, 4):
@@ -427,7 +462,7 @@
                 for n in range(8):
                     put(tmp, n * 8 + 4 * odd + q, v[n])
         for i in range(4):
-            dst[pl.ds(64 + i, 64, stride=16), :] = tmp[pl.ds(2 * i, 64, stride=8), :]
+            dst[pl.ds((base + 4) * 16 + i, 64, stride=16), :] = tmp[pl.ds(2 * i, 64, stride=8), :]
 
     own_a.wait()
     for copy in strips[:4]:
@@ -459,12 +494,12 @@
     to_tiles(fext_rows, l0.f, 0)
     edges = Wide(1, 8, l0.f, 0, 3)
     edges.start()
-    for upper, ref in ((True, l0.up), (False, l0.low)):
-        def body(i, ref=ref, upper=upper):
-            put(tb, i * 16, coarse_faces(*own_pairs(ref, i), 16, upper, 1, None))
-
-        loop(2, body)
-        x_pack(0.25, xgf, 0 if upper else 4, upper)
+
+    def body(i):
+        put(tb, i * 16, coarse_faces(*own_pairs(l0.up, i), 16, 1, None))
+
+    loop(2, body)
+    x_pack(0.25, xgf, True)
     faces_first, faces_second = x_gather(xgf, 1)
     faces_first.start()
     make_coefs(l0, 16)
@@ -477,13 +512,19 @@
         init_down(lv, over_theta)
         step(lv, lv.wa, lv.wb, a1, b1, add="w")
         step(lv, lv.wb, lv.wa, a2, b2, add="x")
-        step(lv, lv.wa, None)
+        if lv in (l0, l1):
+            own_step(lv, lv.wa)
+        else:
+            step(lv, lv.wa, None)
 
     def upward(lv, coarse_at):
         init_up(lv, coarse_at)
         step(lv, lv.wa, lv.wb, None, over_theta, add="xw")
         step(lv, lv.wb, lv.wa, a1, b1)
-        step(lv, lv.wa, None, a2, b2, add="xw", last=True)
+        if lv in (l0, l1):
+            own_step(lv, lv.wa, a2, b2)
+        else:
+            step(lv, lv.wa, None, a2, b2, add="xw", last=True)
 
     def own_sums(lv, i):
         pairs, roots = own_pairs(lv.r, i), own_pairs(lv.root, i)
@@ -495,7 +536,7 @@
         put(tb, i * 16, both(own_sums(l0, i), 1, 1))
 
     loop(2, body)
-    x_pack(0.125, xg1, 0)
+    x_pack(0.125, xg1)
     right_first, right_second = x_gather(xg1, 0)
     right_first.start()
     faces_first.wait_recv()
@@ -514,146 +555,152 @@
 
     for copy in faces_second:
         copy.wait_recv()
-    x_unpack(xgf, 0, l1.up)
-    x_unpack(xgf, 4, l1.low)
-    edges_up, edges_low = Wide(2, 4, l1.up, 0, 3), Wide(3, 4, l1.low, 0, 3)
-    edges_up.start()
-    edges_low.start()
-
-    def second_pack(q, first):
-        start = pl.multiple_of((b // 2) * 64, 64)
-        q[pl.ds(first, 8), :] = jnp.where(lane2 % 2 == 0, tb[pl.ds(start, 8, stride=8), :],
-                                          tb[pl.ds(start + 2, 8, stride=8), :])
-
-    def second_gather(q, yg, zh, n):
-        c = b // 2
-        along = [remote(q, yg.at[c, j], yg_send.at[n, t], yg_recv.at[n, t], gy=lax.rem(j + t, 8)) for t in range(1, 8)]
-        quarters = [remote(yg.at[c], yg.at[c], yc_send.at[n, t], yc_recv.at[n, t], gx=lax.rem(b + 2 * t, 8))
-                    for t in range(1, 4)]
-        halo = [remote(yg.at[3], zh.at[0], h_send.at[n, 0], h_recv.at[n, 0], gz=lax.rem(k + 1, 8)),
-                remote(yg.at[0], zh.at[1], h_send.at[n, 1], h_recv.at[n, 1], gz=lax.rem(k + 7, 8))]
-        return along, quarters, halo
-
-    def second_unpack(yg, zh, first, dst):
-        rows = pl.ds(first, 8)
-        for n in range(8):
-            parts = [zh[0, n, rows, :]] + [yg[c, n, rows, :] for c in range(4)] + [zh[1, n, rows, :]]
-            v = jnp.concatenate(parts, axis=0)
-            dst[pl.ds(2 * n, 48, stride=16), :] = jnp.where(lane2 % 2 == 0, v, roll(v, 1, 1))
-            dst[pl.ds(2 * n + 1, 48, stride=16), :] = jnp.where(lane2 % 2 == 1, v, roll(v, -1, 1))
-
-    for upper, ref in ((True, l1.up), (False, l1.low)):
-        def body(i, ref=ref, upper=upper):
-            put(tb, i * 16, 0.25 * coarse_faces(*own_pairs(ref, i), 32, upper, 1, 1))
-
-        loop(2, body)
-        second_pack(qf, 0 if upper else 8)
-    ygf[b // 2, j] = qf[...]
-    faces_y, faces_c, faces_h = second_gather(qf, ygf, zhf, 0)
-    edges_up.finish()
-    edges_low.finish()
+    x_unpack(xgf, l1.up, 1)
+    edges = Wide(2, 4, l1.up, 1, 4)
+    edges.start()
+
+    c = b // 2
+
+    def second_pack(q):
+        start = pl.multiple_of(c * 64, 64)
+        q[...] = jnp.where(lane2 % 2 == 0, tb[pl.ds(start, 8, stride=8), :], tb[pl.ds(start + 2, 8, stride=8), :])
+
+    class Second:
+        def __init__(self, q, yg, zh, n):
+            yg[c, j] = q[...]
+            self.along = [remote(q, yg.at[c, j], yg_send.at[n, t], yg_recv.at[n, t], gy=lax.rem(j + t, 8))
+                          for t in range(1, 8)]
+            self.quarters = [remote(yg.at[c], yg.at[c], yc_send.at[n, t], yc_recv.at[n, t], gx=lax.rem(b + 2 * t, 8))
+                             for t in range(1, 4)]
+            self.above = [remote(yg.at[3], zh.at[0], h_send.at[n, 0, t], h_recv.at[n, 0],
+                                 gx=lax.rem(b + 2 * t, 8), gz=lax.rem(k + 1, 8)) for t in range(4)]
+            self.below = [remote(yg.at[0], zh.at[1], h_send.at[n, 1, t], h_recv.at[n, 1],
+                                 gx=lax.rem(b + 2 * t, 8), gz=lax.rem(k + 7, 8)) for t in range(4)]
+            self.yg, self.zh = yg, zh
+            for copy in self.along:
+                copy.start()
+
+        def spread(self):
+            for copy in self.along:
+                copy.wait_recv()
+            for copy in self.quarters:
+                copy.start()
+
+            @pl.when(c == 3)
+            def _():
+                for copy in self.above:
+                    copy.start()
+
+            @pl.when(c == 0)
+            def _():
+                for copy in self.below:
+                    copy.start()
+
+        def finish(self, dst, base):
+            for copy in self.quarters + [self.above[0], self.below[0]]:
+                copy.wait_recv()
+            yg, zh = self.yg, self.zh
+            for n in range(8):
+                v = jnp.concatenate([zh[0, n]] + [yg[m, n] for m in range(4)] + [zh[1, n]], axis=0)
+                dst[pl.ds(base * 16 + 2 * n, 48, stride=16), :] = jnp.where(lane2 % 2 == 0, v, roll(v, 1, 1))
+                dst[pl.ds(base * 16 + 2 * n + 1, 48, stride=16), :] = jnp.where(lane2 % 2 == 1, v, roll(v, -1, 1))
+
+        def wait_send(self):
+            for copy in self.along + self.quarters:
+                copy.wait_send()
+
+            @pl.when(c == 3)
+            def _():
+                for copy in self.above:
+                    copy.wait_send()
+
+            @pl.when(c == 0)
+            def _():
+                for copy in self.below:
+                    copy.wait_send()
+
+    def body(i):
+        put(tb, i * 16, 0.25 * coarse_faces(*own_pairs(l1.up, i, 1), 32, 1, 1))
+
+    loop(2, body)
+    second_pack(qf)
+    faces_second_level = Second(qf, ygf, zhf, 0)
+    edges.finish()
     right_first.wait_recv()
     for copy in right_second:
         copy.start()
-    for copy in faces_y:
-        copy.start()
     make_coefs(l1, 32)
 
     for copy in right_second:
         copy.wait_recv()
-    x_unpack(xg1, 0, l1.f)
-    edges = Wide(4, 4, l1.f, 0, 3)
+    x_unpack(xg1, l1.f, 0)
+    edges = Wide(3, 4, l1.f, 0, 3)
     edges.start()
     edges.finish()
-    for copy in faces_y:
-        copy.wait_recv()
-    for copy in faces_c:
-        copy.start()
+    faces_second_level.spread()
     downward(l1)
 
     def body(i):
         put(tb, i * 16, 0.125 * both(both(own_sums(l1, i), 1, 1), 1, 2))
 
     loop(2, body)
-    second_pack(q1, 0)
-    yg1[b // 2, j] = q1[...]
-    right_y, right_c, right_h = second_gather(q1, yg1, zh1, 1)
-    for copy in right_y:
-        copy.start()
-    for copy in faces_c:
-        copy.wait_recv()
-    for copy in faces_h:
-        copy.start()
-    for copy in faces_h:
-        copy.wait_recv()
-    second_unpack(ygf, zhf, 0, l2.up)
-    second_unpack(ygf, zhf, 8, l2.low)
+    second_pack(q1)
+    right_second_level = Second(q1, yg1, zh1, 1)
+    faces_second_level.finish(l2.up, 1)
 
     t = lane % 4
 
-    def third(ref, upper=None):
-        even, odd = (ref[pl.ds(128 + d, 256, stride=2), :].reshape(16, 2, 8, 128) for d in range(2))
-        if upper is None:
+    def third(ref, faces=False):
+        first_row = 144 if faces else 128
+        even, odd = (ref[pl.ds(first_row + d, 256, stride=2), :].reshape(16, 2, 8, 128) for d in range(2))
+        if faces:
+            g = lane // 32
+            first, second = (jnp.where(g == 1, odd[:, d], even[:, d] + odd[:, d]) for d in range(2))
+            v = jnp.where(g == 2, second, first + second)
+            v = 0.25 * jnp.where(g == 0, pick(v, 2, 2), both(v, 2, 2))
+        else:
             roots = [l2.root[pl.ds(128 + d, 256, stride=2), :].reshape(16, 2, 8, 128) for d in range(2)]
             v = even * roots[0] + odd * roots[1]
             v = 0.125 * both(v[:, 0] + v[:, 1], 2, 2)
-        else:
-            g = lane // 32
-            side = odd if upper else even
-            first, second = (jnp.where(g == 1, side[:, d], even[:, d] + odd[:, d]) for d in range(2))
-            v = jnp.where(g == 2, second if upper else first, first + second)
-            v = 0.25 * jnp.where(g == 0, pick(v, 2, 2, upper), both(v, 2, 2))
         v = v.reshape(4, 4, 8, 128)
         out = v[:, 0]
         for u in range(1, 4):
             out = jnp.where(t == u, v[:, u], out)
         return out
 
-    def z_gather(g, n):
-        rows = pl.ds(pl.multiple_of(k * 32, 8), 32)
+    def z_gather(g, n, base):
+        rows = pl.ds(pl.multiple_of((4 * k + base) * 8, 8), 32)
         return [remote(g.at[rows], g.at[rows], zg_send.at[n, u], zg_recv.at[n, u], gz=lax.rem(k + u, 8))
                 for u in range(1, 8)]
 
-    put(l3.up, 4 * k, third(l2.up, True))
-    put(l3.low, 4 * k, third(l2.low, False))
-    third_faces = z_gather(l3.up, 0) + z_gather(l3.low, 1)
+    put(l3.up, 4 * k + 1, third(l2.up, True))
+    third_faces = z_gather(l3.up, 0, 1)
 
     for copy in third_faces:
         copy.start()
     make_coefs(l2, 32)
-    for copy in right_y:
-        copy.wait_recv()
-    for copy in right_c:
-        copy.start()
+    right_second_level.spread()
     for copy in third_faces:
         copy.wait_recv()
     make_coefs(l3, 32)
-    for upper in (True, False):
-        src, dst = (l3.up, l4.up) if upper else (l3.low, l4.low)
-
-        def body(i, src=src, dst=dst, upper=upper):
-            g = lane // 32
-            v = l3.get(src, i)
-            v = jnp.where(g == 2, pick(v, 1, 2, upper), both(v, 1, 2))
-            v = jnp.where(g == 1, pick(v, 1, 1, upper), both(v, 1, 1))
-            l4.put(dst, i, 0.25 * jnp.where(g == 0, pick(v, 4, 2, upper), both(v, 4, 2)))
-
-        l3.loop(body)
-    for copy in right_c:
-        copy.wait_recv()
-    for copy in right_h:
-        copy.start()
+
+    def body(i):
+        g = lane // 32
+        v = l3.get(l3.up, i, 1)
+        v = jnp.where(g == 2, pick(v, 1, 2), both(v, 1, 2))
+        v = jnp.where(g == 1, pick(v, 1, 1), both(v, 1, 1))
+        l4.put(l4.up, i, 0.25 * jnp.where(g == 0, pick(v, 4, 2), both(v, 4, 2)), 1)
+
+    l3.loop(body)
     make_coefs(l4, 32)
-    for copy in right_h:
-        copy.wait_recv()
-    second_unpack(yg1, zh1, 0, l2.f)
-    edges1 = Wide(5, 4, l1.r, 0, 2)
+    right_second_level.finish(l2.f, 0)
+    edges1 = Wide(4, 4, l1.r, 0, 2)
     edges1.start()
     for copy in rx:
         copy.start()
     downward(l2)
     put(l3.f, 4 * k, third(l2.r))
-    third_right = z_gather(l3.f, 2)
+    third_right = z_gather(l3.f, 1, 0)
     for copy in third_right:
         copy.start()
 
@@ -702,7 +749,7 @@
         own = jnp.where(slot // 2 == 1, roll(rxr[0].reshape(8, 8, 128), 2 - 2 * g, 2), own)
         own = jnp.where(slot // 2 == 6, roll(rxr[1].reshape(8, 8, 128), 12 - 2 * g, 2), own)
         put(l0.r, 4 + 8 * g, jnp.concatenate([own, v[:, 8:]], axis=1))
-    edges0 = Wide(6, 8, l0.r, 0, 2)
+    edges0 = Wide(5, 8, l0.r, 0, 2)
     edges0.start()
 
     for i, from_y in ((0, 0), (1, 1), (2, 2), (3, 3), (6, 14), (7, 15)):
@@ -711,7 +758,7 @@
         eb1[pl.ds(2 * i + 1, 48, stride=16), :] = v
     edges1.finish()
     upward(l1, twice(eb1, 6))
-    edges = Wide(7, 4, l1.x, 0, 2)
+    edges = Wide(6, 4, l1.x, 0, 2)
     edges.start()
     edges0.finish()
     edges.finish()
@@ -742,9 +789,10 @@
                 start = d * 64 + v * 16
                 out_ref[pl.ds(v * 64 + y + d, 8, stride=8), :] = turned[start:start + 8]
 
-    for copy in (strips[4:] + [faces_first, right_first] + faces_second + right_second + rx + faces_y + right_y + faces_c
-                 + right_c + faces_h + right_h + third_faces + third_right):
+    for copy in (strips[4:] + [faces_first, right_first] + faces_second + right_second + rx + third_faces + third_right):
         copy.wait_send()
+    faces_second_level.wait_send()
+    right_second_level.wait_send()
 
 
 def solution(mesh):
@@ -757,12 +805,12 @@
             scratch += level_shapes(z, rows)
         scratch += [pltpu.VMEM(shape, F32) for shape in (
             (4, 16, 8, 128), (4, 16, 8, 128),
-            (8, 2, 4, 64, 128), (8, 2, 4, 64, 128), (8, 2, 32, 128), (8, 2, 3, 32, 128),
-            (256, 128), (512, 128), (8, 32, 128), (8, 64, 128), (2, 64, 128), (2, 64, 128),
-            (8, 128), (16, 128), (4, 8, 8, 128), (4, 8, 16, 128), (2, 8, 8, 128), (2, 8, 16, 128), (384, 128), (768, 128), (1152, 128))]
+            (7, 2, 4, 64, 128), (7, 2, 4, 64, 128), (7, 2, 32, 128), (7, 2, 3, 32, 128),
+            (256, 128), (512, 128), (8, 32, 128), (8, 32, 128), (2, 64, 128), (2, 64, 128),
+            (8, 128), (8, 128), (4, 8, 8, 128), (4, 8, 8, 128), (2, 8, 8, 128), (2, 8, 8, 128), (384, 128), (768, 128), (1152, 128))]
         dma = pltpu.SemaphoreType.DMA
         scratch += [dma(shape) for shape in (
-            (2,), (6,), (6,), (8, 8), (8, 8), (2, 4), (2, 4), (2,), (2,), (2, 2), (2, 2), (2, 8), (2, 8), (2, 4), (2, 4), (3, 8), (3, 8))]
+            (2,), (6,), (6,), (7, 8), (7, 8), (2, 4), (2, 4), (2,), (2,), (2, 2, 4), (2, 2), (2, 8), (2, 8), (2, 4), (2, 4), (2, 8), (2, 8))]
         out = pl.pallas_call(
             functools.partial(kernel, nx, ny, nz),
             out_shape=jax.ShapeDtypeStruct((256, 128), F32),

time: 120 us -> 111 us (0.925)
  Pallas kernels: 118 us -> 109 us
    pallas_call x1, Pallas kernels: 118 us -> 109 us  [per_device(): pl.pallas_call(functools.partial(kernel, nx, ny, nz), out_shape=jax.Shape...]
where the time goes in v5:
time: 111 us
  Pallas kernels  109 us (98%)
  local copies, waits for them, and re-layouts  1.57 us (1%)
    pallas_call x1, Pallas kernels, per_device(): pl.pallas_call(functools.partial(kernel, nx, ny, nz), out_shape=jax.Shape...  109 us

profile of v5, /device:TPU:1, one launch (start us, length us, event | category | flops | bytes accessed | tf_op | source)
XLA Modules:
  0.0 110.8 jit_solution(11068847335523855344)
XLA Ops:
  0.0 109.2 %shard_map.28 = f32[256,128]{1,0:T(8,128)} custom-call(f32[4,8,8,128]{3,2,1,0:T(8,128)} %f_hbm.1, f32[3,8,8,128]{3,2,1,0:T(8,128)} %a_hbm.1), custom_call_target="tpu_custom_call" | custom-call | tf_op jit(solution)/shard_map/pallas_call | solution.py:814
  109.2 1.6 %copy.4 = f32[4,8,8,128]{3,2,1,0:T(8,128)} copy(f32[4,8,8,128]{3,2,1,0:T(8,128)} %bitcast.1) | data formatting | bytes 262144

commit v6 on v5

--- a/solution.py
+++ b/solution.py
@@ -249,6 +249,71 @@
         lv.x, lv.x_next = lv.x_next, lv.x
 
 
+def compact(v):
+    v = v.reshape(8, 4, 8, 128)
+    v = [v[n] for n in range(8)]
+    for bit in (iota(2) % 2, (iota(2) // 4) % 2, iota(1) % 2):
+        v = [jnp.where(bit == 0, v[n], v[n + 1]) for n in range(0, len(v), 2)]
+    return v[0]
+
+
+def expand(ref, v):
+    out = [v]
+    for k, axis in ((1, 1), (4, 2), (1, 2)):
+        bit = (iota(axis) // k) % 2
+        out = [jnp.where(bit == m, w, roll(w, k if m == 0 else -k, axis)) for w in out for m in range(2)]
+    for n in range(8):
+        put(ref, 4 * n, out[n])
+
+
+def fourth_neighbours(w):
+    low0, low2, t = iota(2) % 2, (iota(2) // 4) % 2, (iota(2) // 2) % 2
+    last, first = w[3:], w[:1]
+    up = jnp.where(low0 == 0, roll(first, -1, 2),
+                   jnp.where(low2 == 0, roll(first, -3, 2), roll(roll(first, 5, 2), -1, 1)))
+    down = jnp.where(low0 == 1, roll(last, 1, 2),
+                     jnp.where(low2 == 1, roll(last, 3, 2), roll(roll(last, -5, 2), 1, 1)))
+    after, before = jnp.concatenate([w[1:], up], axis=0), jnp.concatenate([down, w[:3]], axis=0)
+    return [roll(w, 8, 2), roll(w, -8, 2), roll(w, 2, 1), roll(w, -2, 1),
+            jnp.where(t == 1, roll(w, 2, 2), roll(before, -2, 2)),
+            jnp.where(t == 0, roll(w, -2, 2), roll(after, 2, 2))]
+
+
+def fourth_coefs(lv, up):
+    x_low, _, y_low, _, z_low, _ = fourth_neighbours(up)
+    lows = [jnp.where(iota(2) % 32 < 8, 0.0, x_low), y_low, z_low]
+    g = iota(2) // 32
+    faces = []
+    for k in range(3):
+        for value in (lows[k], up):
+            out = value
+            for to in range(4):
+                if to != k:
+                    out = jnp.where(g == to, roll(value, 32 * (to - k), 2), out)
+            faces.append(out)
+    total = faces[0] + faces[1] + faces[2] + faces[3] + faces[4] + faces[5]
+    scale = lax.rsqrt(total)
+    put(lv.scale, 0, scale)
+    put(lv.root, 0, scale * total)
+    for k in range(6):
+        put(lv.coef, 4 * k, scale * scale * faces[k])
+
+
+def fourth_solve(lv, f):
+    over_theta, steps = SOLVE
+    coefs = [slots(lv.coef, 4 * k, 4, 8) for k in range(6)]
+    r = slots(lv.scale, 0, 4, 8) * f
+    w = x = r * over_theta
+    for alpha, beta in steps:
+        total = None
+        for coef, value in zip(coefs, fourth_neighbours(w)):
+            total = coef * value if total is None else total + coef * value
+        r = r - ((1.0 + SHIFT) * w - total)
+        w = alpha * w + beta * r
+        x = x + w
+    return x * slots(lv.root, 0, 4, 8)
+
+
 def kernel(nx, ny, nz, f_hbm, a_hbm, out_ref, *scratch):
     refs = list(scratch)
 
@@ -419,11 +484,15 @@
     fext_rows, aext_rows = fext.reshape(512, 128), aext.reshape(512, 128)
 
     def x_gather(xg, n):
-        first = remote(xg.at[b], xg.at[b], xg_send.at[n, 0], xg_recv.at[n, 0], gx=b + 1 - 2 * lax.rem(b, 2))
-        pair = pl.ds((b // 2) * 2, 2)
-        second = [remote(xg.at[pair], xg.at[pair], xg_send.at[n, t], xg_recv.at[n, t], gx=lax.rem(b + 2 * t, 8))
-                  for t in range(1, 4)]
-        return first, second
+        other = b + 1 - 2 * lax.rem(b, 2)
+        first = remote(xg.at[b], xg.at[b], xg_send.at[n, 0], xg_recv.at[n, 0], gx=other)
+        early = [remote(xg.at[b], xg.at[b], xg_send.at[n, t], xg_recv.at[n, t], gx=lax.rem(b + 2 * t, 8))
+                 for t in range(1, 4)]
+        second = [remote(xg.at[other], xg.at[other], xg_send.at[n, 3 + t], xg_recv.at[n, 3 + t],
+                         gx=lax.rem(b + 2 * t, 8)) for t in range(1, 4)]
+        for copy in [first] + early:
+            copy.start()
+        return first, early, second
 
     def x_pack(weight, xg, faces=False):
         source = lax.broadcasted_iota(jnp.int32, (128, 256), 0)
@@ -500,8 +569,7 @@
 
     loop(2, body)
     x_pack(0.25, xgf, True)
-    faces_first, faces_second = x_gather(xgf, 1)
-    faces_first.start()
+    faces_first, faces_early, faces_second = x_gather(xgf, 1)
     make_coefs(l0, 16)
 
     edges.finish()
@@ -537,8 +605,7 @@
 
     loop(2, body)
     x_pack(0.125, xg1)
-    right_first, right_second = x_gather(xg1, 0)
-    right_first.start()
+    right_first, right_early, right_second = x_gather(xg1, 0)
     faces_first.wait_recv()
     for copy in faces_second:
         copy.start()
@@ -553,7 +620,7 @@
     rx = [remote(rxs.at[0], rxr.at[0], rx_send.at[0], rx_recv.at[0], gx=b_up),
           remote(rxs.at[1], rxr.at[1], rx_send.at[1], rx_recv.at[1], gx=b_down)]
 
-    for copy in faces_second:
+    for copy in faces_early + faces_second:
         copy.wait_recv()
     x_unpack(xgf, l1.up, 1)
     edges = Wide(2, 4, l1.up, 1, 4)
@@ -631,7 +698,7 @@
         copy.start()
     make_coefs(l1, 32)
 
-    for copy in right_second:
+    for copy in right_early + right_second:
         copy.wait_recv()
     x_unpack(xg1, l1.f, 0)
     edges = Wide(3, 4, l1.f, 0, 3)
@@ -680,45 +747,34 @@
         copy.start()
     make_coefs(l2, 32)
     right_second_level.spread()
+    for copy in rx:
+        copy.start()
     for copy in third_faces:
         copy.wait_recv()
     make_coefs(l3, 32)
 
-    def body(i):
-        g = lane // 32
-        v = l3.get(l3.up, i, 1)
-        v = jnp.where(g == 2, pick(v, 1, 2), both(v, 1, 2))
-        v = jnp.where(g == 1, pick(v, 1, 1), both(v, 1, 1))
-        l4.put(l4.up, i, 0.25 * jnp.where(g == 0, pick(v, 4, 2), both(v, 4, 2)), 1)
-
-    l3.loop(body)
-    make_coefs(l4, 32)
+    group = lane // 32
+    v = slots(l3.up, 1, 32, 8)
+    v = jnp.where(group == 2, pick(v, 1, 2), both(v, 1, 2))
+    v = jnp.where(group == 1, pick(v, 1, 1), both(v, 1, 1))
+    fourth_coefs(l4, 0.25 * compact(jnp.where(group == 0, pick(v, 4, 2), both(v, 4, 2))))
     right_second_level.finish(l2.f, 0)
     edges1 = Wide(4, 4, l1.r, 0, 2)
     edges1.start()
-    for copy in rx:
-        copy.start()
     downward(l2)
     put(l3.f, 4 * k, third(l2.r))
     third_right = z_gather(l3.f, 1, 0)
     for copy in third_right:
         copy.start()
 
+    edges1.finish()
     for copy in third_right:
         copy.wait_recv()
 
     downward(l3)
 
-    def body(i):
-        l4.put(l4.f, i, 0.125 * both(both(both(l3.get(l3.r, i) * l3.get(l3.root, i), 1, 2), 1, 1), 4, 2))
-
-    l3.loop(body)
-    solve_theta, solve_steps = SOLVE
-    init_down(l4, solve_theta)
-    w, w_next = l4.wa, l4.wb
-    for n, (alpha, beta) in enumerate(solve_steps):
-        step(l4, w, w_next, alpha, beta, add="x" if n else "w", last=n == len(solve_steps) - 1)
-        w, w_next = w_next, w
+    v = slots(l3.r, 0, 32, 8) * slots(l3.root, 0, 32, 8)
+    expand(l4.x, fourth_solve(l4, 0.125 * compact(both(both(both(v, 1, 2), 1, 1), 4, 2))))
     upward(l3, lambda i: l4.get(l4.x, i))
 
     for q in range(6):
@@ -756,7 +812,6 @@
         v = l2.x[pl.ds(lax.rem(2 * j + from_y, 16), 48, stride=16), :]
         eb1[pl.ds(2 * i, 48, stride=16), :] = v
         eb1[pl.ds(2 * i + 1, 48, stride=16), :] = v
-    edges1.finish()
     upward(l1, twice(eb1, 6))
     edges = Wide(6, 4, l1.x, 0, 2)
     edges.start()
@@ -789,7 +844,8 @@
                 start = d * 64 + v * 16
                 out_ref[pl.ds(v * 64 + y + d, 8, stride=8), :] = turned[start:start + 8]
 
-    for copy in (strips[4:] + [faces_first, right_first] + faces_second + right_second + rx + third_faces + third_right):
+    for copy in (strips[4:] + [faces_first, right_first] + faces_early + right_early + faces_second + right_second + rx
+                 + third_faces + third_right):
         copy.wait_send()
     faces_second_level.wait_send()
     right_second_level.wait_send()
@@ -810,7 +866,7 @@
             (8, 128), (8, 128), (4, 8, 8, 128), (4, 8, 8, 128), (2, 8, 8, 128), (2, 8, 8, 128), (384, 128), (768, 128), (1152, 128))]
         dma = pltpu.SemaphoreType.DMA
         scratch += [dma(shape) for shape in (
-            (2,), (6,), (6,), (7, 8), (7, 8), (2, 4), (2, 4), (2,), (2,), (2, 2, 4), (2, 2), (2, 8), (2, 8), (2, 4), (2, 4), (2, 8), (2, 8))]
+            (2,), (6,), (6,), (7, 8), (7, 8), (2, 7), (2, 7), (2,), (2,), (2, 2, 4), (2, 2), (2, 8), (2, 8), (2, 4), (2, 4), (2, 8), (2, 8))]
         out = pl.pallas_call(
             functools.partial(kernel, nx, ny, nz),
             out_shape=jax.ShapeDtypeStruct((256, 128), F32),

time: 111 us -> 106 us (0.955)
  Pallas kernels: 109 us -> 105 us
    pallas_call x1, Pallas kernels: 109 us -> 105 us  [per_device(): pl.pallas_call(functools.partial(kernel, nx, ny, nz), out_shape=jax.Shape...]
where the time goes in v6:
time: 106 us
  Pallas kernels  105 us (99%)
  local copies, waits for them, and re-layouts  1.57 us (1%)
    pallas_call x1, Pallas kernels, per_device(): pl.pallas_call(functools.partial(kernel, nx, ny, nz), out_shape=jax.Shape...  105 us

profile of v6, /device:TPU:1, one launch (start us, length us, event | category | flops | bytes accessed | tf_op | source)
XLA Modules:
  0.0 106.2 jit_solution(12486397154239595382)
XLA Ops:
  0.0 104.7 %shard_map.28 = f32[256,128]{1,0:T(8,128)} custom-call(f32[4,8,8,128]{3,2,1,0:T(8,128)} %f_hbm.1, f32[3,8,8,128]{3,2,1,0:T(8,128)} %a_hbm.1), custom_call_target="tpu_custom_call" | custom-call | tf_op jit(solution)/shard_map/pallas_call | solution.py:870
  104.7 1.6 %copy.4 = f32[4,8,8,128]{3,2,1,0:T(8,128)} copy(f32[4,8,8,128]{3,2,1,0:T(8,128)} %bitcast.1) | data formatting | bytes 262144

commit v7 on v6

--- a/solution.py
+++ b/solution.py
@@ -105,7 +105,7 @@
         put(ref, i * self.ch + offset, value)
 
 
-LEVELS = ((72, 16, 1, 1, 0), (72, 16, 1, 1, 0), (48, 16, 1, 2, 0), (32, 8, 1, 4, 1), (32, 8, 2, 8, 2))
+LEVELS = ((72, 16, 1, 1, 0), (72, 16, 1, 1, 0), (24, 16, 1, 2, 0), (32, 8, 1, 4, 1), (32, 8, 2, 8, 2))
 
 
 def level_shapes(z, rows):
@@ -113,6 +113,12 @@
     pad = (z + 2) * rows
     return [pltpu.VMEM((6 * n, 128), F32)] + [pltpu.VMEM((n, 128), F32)] * 5 + [pltpu.VMEM((pad, 128), F32)] * 4 + [
         pltpu.VMEM((n, 128), F32)] * 2
+
+
+def join_halves(ref):
+    odd = iota(2, (1, 16, 128)) % 2 == 1
+    put(ref, 0, jnp.where(odd, roll(slots(ref, 24, 1), 1, 2), 0.0))
+    put(ref, 25, jnp.where(odd, 0.0, roll(slots(ref, 1, 1), -1, 2)))
 
 
 def neighbours(lv, w_ref, i):
@@ -146,6 +152,9 @@
 
 
 def step(lv, w_ref, w_next, alpha=None, beta=None, add="", last=False):
+    if lv.z == 24:
+        join_halves(w_ref)
+
     def body(i):
         w, *near = neighbours(lv, w_ref, i)
         total = None
@@ -182,6 +191,9 @@
             if to != k:
                 out = jnp.where(g == to, roll(value, group * (to - k), 2), out)
         return out
+
+    if lv.z == 24:
+        join_halves(lv.up)
 
     def body(i):
         if group == 16:
@@ -669,8 +681,9 @@
             yg, zh = self.yg, self.zh
             for n in range(8):
                 v = jnp.concatenate([zh[0, n]] + [yg[m, n] for m in range(4)] + [zh[1, n]], axis=0)
-                dst[pl.ds(base * 16 + 2 * n, 48, stride=16), :] = jnp.where(lane2 % 2 == 0, v, roll(v, 1, 1))
-                dst[pl.ds(base * 16 + 2 * n + 1, 48, stride=16), :] = jnp.where(lane2 % 2 == 1, v, roll(v, -1, 1))
+                low, high = v[:24], v[24:]
+                dst[pl.ds(base * 16 + 2 * n, 24, stride=16), :] = jnp.where(lane2 % 2 == 0, low, roll(high, 1, 1))
+                dst[pl.ds(base * 16 + 2 * n + 1, 24, stride=16), :] = jnp.where(lane2 % 2 == 0, roll(low, -1, 1), high)
 
         def wait_send(self):
             for copy in self.along + self.quarters:
@@ -718,17 +731,26 @@
     t = lane % 4
 
     def third(ref, faces=False):
-        first_row = 144 if faces else 128
-        even, odd = (ref[pl.ds(first_row + d, 256, stride=2), :].reshape(16, 2, 8, 128) for d in range(2))
+        g, odd_lane = lane // 32, lane % 2 == 1
+
+        def rows(values, d):
+            return values[pl.ds((16 if faces else 0) + d, 192, stride=2), :].reshape(24, 8, 128)
+
         if faces:
-            g = lane // 32
-            first, second = (jnp.where(g == 1, odd[:, d], even[:, d] + odd[:, d]) for d in range(2))
-            v = jnp.where(g == 2, second, first + second)
+            v = jnp.where(g == 1, rows(ref, 1), rows(ref, 0) + rows(ref, 1))
+        else:
+            v = rows(ref, 0) * rows(l2.root, 0) + rows(ref, 1) * rows(l2.root, 1)
+        halves = []
+        for part in (v[8:], v[:16]):
+            part = part.reshape(8, 2, 8, 128)
+            both_z = part[:, 0] + part[:, 1]
+            halves.append(jnp.where(g == 2, part[:, 1], both_z) if faces else both_z)
+        v = jnp.concatenate([jnp.where(odd_lane, roll(halves[0], 1, 2), halves[0]),
+                             jnp.where(odd_lane, halves[1], roll(halves[1], -1, 2))], axis=0)
+        if faces:
             v = 0.25 * jnp.where(g == 0, pick(v, 2, 2), both(v, 2, 2))
         else:
-            roots = [l2.root[pl.ds(128 + d, 256, stride=2), :].reshape(16, 2, 8, 128) for d in range(2)]
-            v = even * roots[0] + odd * roots[1]
-            v = 0.125 * both(v[:, 0] + v[:, 1], 2, 2)
+            v = 0.125 * both(v, 2, 2)
         v = v.reshape(4, 4, 8, 128)
         out = v[:, 0]
         for u in range(1, 4):
@@ -795,7 +817,11 @@
 
         return chunk
 
-    upward(l2, twice(eb2, 0))
+    def second_chunk(i):
+        v = jnp.where(lane16 % 2 == 0, slots(eb2, i * 4, 4), slots(eb2, i * 4 + 12, 4))
+        return jnp.broadcast_to(v[:, None], (4, 2, 16, 128)).reshape(8, 16, 128)
+
+    upward(l2, second_chunk)
 
     for copy in rx:
         copy.wait_recv()
@@ -809,9 +835,11 @@
     edges0.start()
 
     for i, from_y in ((0, 0), (1, 1), (2, 2), (3, 3), (6, 14), (7, 15)):
-        v = l2.x[pl.ds(lax.rem(2 * j + from_y, 16), 48, stride=16), :]
-        eb1[pl.ds(2 * i, 48, stride=16), :] = v
-        eb1[pl.ds(2 * i + 1, 48, stride=16), :] = v
+        v = l2.x[pl.ds(lax.rem(2 * j + from_y, 16), 24, stride=16), :]
+        low, high = jnp.where(lane2 % 2 == 0, v, roll(v, 1, 1)), jnp.where(lane2 % 2 == 1, v, roll(v, -1, 1))
+        for d in range(2):
+            eb1[pl.ds(2 * i + d, 24, stride=16), :] = low
+            eb1[pl.ds(2 * i + d + 384, 24, stride=16), :] = high
     upward(l1, twice(eb1, 6))
     edges = Wide(6, 4, l1.x, 0, 2)
     edges.start()

time: 106 us -> 106 us (level)
  no operation moved by 1% of the time
where the time goes in v7:
time: 106 us
  Pallas kernels  104 us (98%)
  local copies, waits for them, and re-layouts  1.57 us (1%)
    pallas_call x1, Pallas kernels, per_device(): pl.pallas_call(functools.partial(kernel, nx, ny, nz), out_shape=jax.Shape...  104 us

profile of v7, /device:TPU:1, one launch (start us, length us, event | category | flops | bytes accessed | tf_op | source)
XLA Modules:
  0.0 105.9 jit_solution(7838621632178488398)
XLA Ops:
  0.0 104.3 %shard_map.28 = f32[256,128]{1,0:T(8,128)} custom-call(f32[4,8,8,128]{3,2,1,0:T(8,128)} %f_hbm.1, f32[3,8,8,128]{3,2,1,0:T(8,128)} %a_hbm.1), custom_call_target="tpu_custom_call" | custom-call | tf_op jit(solution)/shard_map/pallas_call | solution.py:898
  104.3 1.6 %copy.4 = f32[4,8,8,128]{3,2,1,0:T(8,128)} copy(f32[4,8,8,128]{3,2,1,0:T(8,128)} %bitcast.1) | data formatting | bytes 262144

commit v8 on v7

--- a/solution.py
+++ b/solution.py
@@ -390,11 +390,7 @@
         remote(f_hbm.at[:, pl.ds(0, 3)], fext.at[:, pl.ds(12, 3)],
                strip_send.at[3], strip_recv.at[3], gx=b_down),
     ]
-    for copy in strips[:4]:
-        copy.start()
-    for copy in strips[:4]:
-        copy.wait_send()
-    for copy in strips[4:]:
+    for copy in strips:
         copy.start()
 
     class Wide:
@@ -872,7 +868,7 @@
                 start = d * 64 + v * 16
                 out_ref[pl.ds(v * 64 + y + d, 8, stride=8), :] = turned[start:start + 8]
 
-    for copy in (strips[4:] + [faces_first, right_first] + faces_early + right_early + faces_second + right_second + rx
+    for copy in (strips + [faces_first, right_first] + faces_early + right_early + faces_second + right_second + rx
                  + third_faces + third_right):
         copy.wait_send()
     faces_second_level.wait_send()

time: 106 us -> 106 us (level)
  no operation moved by 1% of the time
where the time goes in v8:
time: 106 us
  Pallas kernels  104 us (98%)
  local copies, waits for them, and re-layouts  1.57 us (1%)
    pallas_call x1, Pallas kernels, per_device(): pl.pallas_call(functools.partial(kernel, nx, ny, nz), out_shape=jax.Shape...  104 us

profile of v8, /device:TPU:1, one launch (start us, length us, event | category | flops | bytes accessed | tf_op | source)
XLA Modules:
  0.0 106.1 jit_solution(2544725709713944599)
XLA Ops:
  0.0 104.5 %shard_map.28 = f32[256,128]{1,0:T(8,128)} custom-call(f32[4,8,8,128]{3,2,1,0:T(8,128)} %f_hbm.1, f32[3,8,8,128]{3,2,1,0:T(8,128)} %a_hbm.1), custom_call_target="tpu_custom_call" | custom-call | tf_op jit(solution)/shard_map/pallas_call | solution.py:894
  104.5 1.6 %copy.4 = f32[4,8,8,128]{3,2,1,0:T(8,128)} copy(f32[4,8,8,128]{3,2,1,0:T(8,128)} %bitcast.1) | data formatting | bytes 262144

commit v9 on v7

--- a/solution.py
+++ b/solution.py
@@ -82,7 +82,7 @@
     def __init__(self, z, rows, sy, sx, mode, refs):
         self.z, self.rows, self.sy, self.sx, self.mode = z, rows, sy, sx, mode
         self.ch = 128 // rows
-        self.parts = z // self.ch if rows == 8 else 3
+        self.parts = z // self.ch
         (self.coef, self.scale, self.root, self.f, self.r, self.x, self.wa, self.wb, self.up, self.low,
          self.r_next, self.x_next) = refs
 

time: 106 us -> 104 us (0.981)
  Pallas kernels: 104 us -> 102 us
    pallas_call x1, Pallas kernels: 104 us -> 102 us  [per_device(): pl.pallas_call(functools.partial(kernel, nx, ny, nz), out_shape=jax.Shape...]
where the time goes in v9:
time: 104 us
  Pallas kernels  102 us (98%)
  local copies, waits for them, and re-layouts  1.57 us (2%)
    pallas_call x1, Pallas kernels, per_device(): pl.pallas_call(functools.partial(kernel, nx, ny, nz), out_shape=jax.Shape...  102 us

profile of v9, /device:TPU:1, one launch (start us, length us, event | category | flops | bytes accessed | tf_op | source)
XLA Modules:
  0.0 104.1 jit_solution(11138058878647861881)
XLA Ops:
  0.0 102.5 %shard_map.28 = f32[256,128]{1,0:T(8,128)} custom-call(f32[4,8,8,128]{3,2,1,0:T(8,128)} %f_hbm.1, f32[3,8,8,128]{3,2,1,0:T(8,128)} %a_hbm.1), custom_call_target="tpu_custom_call" | custom-call | tf_op jit(solution)/shard_map/pallas_call | solution.py:898
  102.5 1.6 %copy.4 = f32[4,8,8,128]{3,2,1,0:T(8,128)} copy(f32[4,8,8,128]{3,2,1,0:T(8,128)} %bitcast.1) | data formatting | bytes 262144
